TPU v7x, 256 devices: a whole 4x4x8 slice. The times are simulated.
256 devices in a mesh: pair: 64 (over z, y, core), cuts: 4 (over x).
Axes of the slice: x: 4, y: 4, z: 8, core: 2. Of those that a mesh axis runs over, the one named last changes fastest.
Arguments:
- t2_tiles: bfloat16 [24576, 128, 128], P(('pair', 'cuts')), may hold values from -6 to 6
- kc_tile: int32 [24576], P(('pair', 'cuts')), may hold values from 0 to 63
- jb_tile: int32 [24576], P(('pair', 'cuts')), may hold values from 0 to 1
- tile_owner: int32 [24576, 1], P(('pair', 'cuts')), may hold values from 0 to 63; in each aligned block of 96 rows (0 to 95, 96 to 191, ...) at most 3 rows name the same one
- w_slices: bfloat16 [1024, 32768], P(None, 'cuts'), may hold values from -0.0390625 to 0.0390625
Outputs:
- cycle: bfloat16 [1024, 16384], P('cuts', 'pair')
Inputs may be any that keep to these rules, and one draw needn't show every extreme that they name: `tile_owner`: in the rows of one device no owner is named more than 3 times, and in some device some owner is named exactly 3 times.
All inputs are finite; a program needn't handle non-finite values.
Results may differ from a plain program's by a relative error of at most 0.001.
Values may be sent and summed in bfloat16 or wider, within the bound.
No kernel may reach another device: no remote copies, remote signals or barrier semaphores. Data moves between devices by JAX's collectives and lax.ppermute only.
A program may use at most 192 MiB of HBM per device.

v0:
```python
import math

import jax
import jax.numpy as jnp
from jax import lax
from jax.sharding import PartitionSpec as P

SP = 2


def contract(w_blocks, tiles_in, ids_in, columns):
    count = tiles_in.shape[0]
    block_size = math.gcd(count, 32)
    row_count = w_blocks.shape[0]
    tile_size = tiles_in.shape[-1]
    grouped_tiles = tiles_in.reshape(count // block_size, block_size, tile_size, tile_size)
    grouped_ids = ids_in.reshape(count // block_size, block_size, 2)

    def one_block(running, pieces):
        tile_block, id_block = pieces
        picked = jnp.take(w_blocks, id_block[:, 0], axis=1)
        product = jnp.einsum("rna,nab->rnb", picked, tile_block, preferred_element_type=jnp.float32)
        running = running.at[:, id_block[:, 1], :].add(product)
        return (running, None)

    start_value = jnp.zeros((row_count, columns, tile_size), jnp.float32)
    total, _ = lax.scan(one_block, start_value, (grouped_tiles, grouped_ids))
    return total.reshape(row_count, columns * tile_size)


def local(t2_tiles, kc_tile, jb_tile, tile_owner, w_slices):
    pair_count = lax.axis_size("pair")
    held_count = t2_tiles.shape[0]
    tile_size = t2_tiles.shape[1]
    capacity = max(2, (3 * held_count + 2 * pair_count - 1) // (2 * pair_count))
    slot_total = pair_count * capacity
    owners = tile_owner[:, 0]
    member = (owners[:, None] == jnp.arange(pair_count, dtype=jnp.int32)[None, :]).astype(jnp.int32)
    before = jnp.cumsum(member, axis=0) - member
    slot_rank = jnp.sum(before * member, axis=1)
    slot_index = owners * capacity + slot_rank
    send_tiles = (
        jnp.zeros((slot_total, tile_size, tile_size), t2_tiles.dtype).at[slot_index].set(t2_tiles)
    )
    send_ids = (
        jnp.zeros((slot_total, 2), jnp.int32)
        .at[slot_index]
        .set(jnp.stack([kc_tile, jb_tile], axis=1))
    )
    row_count = w_slices.shape[0]
    w_blocks = w_slices.reshape(row_count, w_slices.shape[1] // tile_size, tile_size)
    recv_tiles, recv_ids = (
        lax.all_to_all(send_tiles, "pair", split_axis=0, concat_axis=0, tiled=True),
        lax.all_to_all(send_ids, "pair", split_axis=0, concat_axis=0, tiled=True),
    )
    partial_sum = contract(w_blocks, recv_tiles, recv_ids, SP)
    summed = lax.psum(partial_sum, "cuts")
    part_rows = row_count // lax.axis_size("cuts")
    own_rows = lax.dynamic_slice_in_dim(summed, lax.axis_index("cuts") * part_rows, part_rows, 0)
    return own_rows.astype(jnp.bfloat16)


def solution(mesh):
    return jax.shard_map(
        local,
        mesh=mesh,
        in_specs=(
            P(("pair", "cuts"), None, None),
            P(("pair", "cuts")),
            P(("pair", "cuts")),
            P(("pair", "cuts"), None),
            P(None, "cuts"),
        ),
        out_specs=P("cuts", "pair"),
        check_vma=False,
    )
```

profile of v0, /device:TPU:32, one launch (start us, length us, event | category | flops | bytes accessed | tf_op | source)
XLA Modules:
  0.0 479.2 jit_solution(7362640685067039530)
XLA Ops:
  5.1 11.8 %all-to-all-start = ((s32[64,3,2]{1,2,0:T(2,128)}), s32[64,3,2]{1,2,0:T(2,128)S(1)}, u32[]{:S(2)}, u32[]{:S(2)}) async-start(s32[64,3,2]{1,2,0:T(2,128)} %copy.20), calls=%async_computation | async-start | bytes 131072 | tf_op jit(solution)/shard_map/all_to_all | solution.py:54
  21.0 12.7 %scatter_fusion.1 = bf16[192,128,128]{2,1,0:T(8,128)(2,1)} fusion(bf16[192,128,128]{2,1,0:T(8,128)(2,1)} %broadcast_in_dim.25, s32[96]{0:T(128)S(1)} %fusion.14, bf16[96,128,128]{2,1,0:T(8,128)(2,1)S(1)} %copy-done), kind=kCustom, calls=%fused_computation.3 | custom fusion | bytes 9437568 | tf_op jit(solution)/shard_map/scatter | solution.py:43
  44.2 22.4 %copy.22 = bf16[1024,8192]{0,1:T(8,128)(2,1)} copy(bf16[1024,8192]{1,0:T(8,128)(2,1)} %param.11) | data formatting | bytes 33554432 | tf_op args[4]
  66.6 22.4 %copy.24 = bf16[1024,64,128]{2,0,1:T(8,128)(2,1)} copy(bf16[1024,64,128]{0,2,1:T(8,128)(2,1)} %bitcast.45) | data formatting | bytes 33554432 | tf_op jit(solution)/shard_map/while | solution.py:27
  89.1 95.7 %all-to-all-done.1 = bf16[192,128,128]{2,1,0:T(8,128)(2,1)} async-done(((bf16[192,128,128]{2,1,0:T(8,128)(2,1)}), bf16[192,128,128]{2,1,0:T(8,128)(2,1)}, u32[]{:S(2)}, u32[]{:S(2)}) %all-to-all-start.1) | async-done | bytes 6291488 | tf_op jit(solution)/shard_map/all_to_all | solution.py:53
  184.9 260.5 %while.10 = (s32[]{:T(128)}, f32[1024,2,128]{2,0,1:T(8,128)S(1)}, s32[6,32,2]{1,0,2:T(8,128)S(1)}, bf16[6,32,128,128]{3,2,1,0:T(8,128)(2,1)}, bf16[1024,64,128]{2,0,1:T(8,128)(2,1)}, /*index=5*/s32[]{:T(128)}) while((s32[]{:T(128)}, f32[1024,2,128]{2,0,1:T(8,128)S(1)}, s32[6,32,2]{1,0,2:T(8,128)S(1)}, bf16[6,32,128,128]{3,2,1,0:T(8,128)(2,1)}, ...), condition=%wide.region_6.7_spmd, body=%wide.region_4.6_spmd.sunk | while | flops 1082131840 | bytes 93329544 | solution.py:27
  185.0 10.7 %gather_fusion = bf16[32,1024,128]{2,1,0:T(8,128)(2,1)} fusion(bf16[1024,64,128]{2,0,1:T(8,128)(2,1)} %get-tuple-element.111, s32[1024]{0:T(1024)S(1)} %pad_clamp_fusion.2), kind=kCustom, calls=%fused_computation.clone.1 | custom fusion | bytes 16777344 | tf_op jit(solution)/shard_map/while/body/eval_jaxpr/jit(_take)/gather | solution.py:21
  195.7 11.7 %fusion.23 = f32[32,1024,128]{2,1,0:T(8,128)} fusion(bf16[32,1024,128]{2,1,0:T(8,128)(2,1)} %gather_fusion, pred[32]{0:T(512)(128)(4,1)S(1)} %and_bitcast_fusion.2, bf16[6,32,128,128]{3,2,1,0:T(8,128)(2,1)} %get-tuple-element.110, s32[]{:T(128)} %get-tuple-element.101), kind=kOutput, calls=%fused_computation.4.clone.1 | convolution fusion | flops 1077936128 | bytes 26214944 | tf_op jit(solution)/shard_map/while/body/eval_jaxpr/rna,nab->rnb/dot_general | solution.py:22
  207.4 20.9 %scatter_fusion = f32[1024,2,128]{2,0,1:T(8,128)S(1)} fusion(f32[1024,2,128]{2,0,1:T(8,128)S(1)} %get-tuple-element.102, s32[32]{0:T(128)S(1)} %get-tuple-element.93, f32[32,1024,128]{2,1,0:T(8,128)} %fusion.23), kind=kCustom, calls=%fused_computation.1.clone.1 | custom fusion | flops 4194304 | bytes 50331776 | tf_op jit(solution)/shard_map/while/body/eval_jaxpr/scatter-add | solution.py:23
  228.4 10.7 %gather_fusion = bf16[32,1024,128]{2,1,0:T(8,128)(2,1)} fusion(bf16[1024,64,128]{2,0,1:T(8,128)(2,1)} %get-tuple-element.111, s32[1024]{0:T(1024)S(1)} %pad_clamp_fusion.2), kind=kCustom, calls=%fused_computation.clone.1 | custom fusion | bytes 16777344 | tf_op jit(solution)/shard_map/while/body/eval_jaxpr/jit(_take)/gather | solution.py:21
  239.1 11.7 %fusion.23 = f32[32,1024,128]{2,1,0:T(8,128)} fusion(bf16[32,1024,128]{2,1,0:T(8,128)(2,1)} %gather_fusion, pred[32]{0:T(512)(128)(4,1)S(1)} %and_bitcast_fusion.2, bf16[6,32,128,128]{3,2,1,0:T(8,128)(2,1)} %get-tuple-element.110, s32[]{:T(128)} %get-tuple-element.101), kind=kOutput, calls=%fused_computation.4.clone.1 | convolution fusion | flops 1077936128 | bytes 26214944 | tf_op jit(solution)/shard_map/while/body/eval_jaxpr/rna,nab->rnb/dot_general | solution.py:22
  250.8 20.9 %scatter_fusion = f32[1024,2,128]{2,0,1:T(8,128)S(1)} fusion(f32[1024,2,128]{2,0,1:T(8,128)S(1)} %get-tuple-element.102, s32[32]{0:T(128)S(1)} %get-tuple-element.93, f32[32,1024,128]{2,1,0:T(8,128)} %fusion.23), kind=kCustom, calls=%fused_computation.1.clone.1 | custom fusion | flops 4194304 | bytes 50331776 | tf_op jit(solution)/shard_map/while/body/eval_jaxpr/scatter-add | solution.py:23
  271.8 10.6 %gather_fusion = bf16[32,1024,128]{2,1,0:T(8,128)(2,1)} fusion(bf16[1024,64,128]{2,0,1:T(8,128)(2,1)} %get-tuple-element.111, s32[1024]{0:T(1024)S(1)} %pad_clamp_fusion.2), kind=kCustom, calls=%fused_computation.clone.1 | custom fusion | bytes 16777344 | tf_op jit(solution)/shard_map/while/body/eval_jaxpr/jit(_take)/gather | solution.py:21
  282.4 11.7 %fusion.23 = f32[32,1024,128]{2,1,0:T(8,128)} fusion(bf16[32,1024,128]{2,1,0:T(8,128)(2,1)} %gather_fusion, pred[32]{0:T(512)(128)(4,1)S(1)} %and_bitcast_fusion.2, bf16[6,32,128,128]{3,2,1,0:T(8,128)(2,1)} %get-tuple-element.110, s32[]{:T(128)} %get-tuple-element.101), kind=kOutput, calls=%fused_computation.4.clone.1 | convolution fusion | flops 1077936128 | bytes 26214944 | tf_op jit(solution)/shard_map/while/body/eval_jaxpr/rna,nab->rnb/dot_general | solution.py:22
  294.1 21.0 %scatter_fusion = f32[1024,2,128]{2,0,1:T(8,128)S(1)} fusion(f32[1024,2,128]{2,0,1:T(8,128)S(1)} %get-tuple-element.102, s32[32]{0:T(128)S(1)} %get-tuple-element.93, f32[32,1024,128]{2,1,0:T(8,128)} %fusion.23), kind=kCustom, calls=%fused_computation.1.clone.1 | custom fusion | flops 4194304 | bytes 50331776 | tf_op jit(solution)/shard_map/while/body/eval_jaxpr/scatter-add | solution.py:23
  315.1 10.7 %gather_fusion = bf16[32,1024,128]{2,1,0:T(8,128)(2,1)} fusion(bf16[1024,64,128]{2,0,1:T(8,128)(2,1)} %get-tuple-element.111, s32[1024]{0:T(1024)S(1)} %pad_clamp_fusion.2), kind=kCustom, calls=%fused_computation.clone.1 | custom fusion | bytes 16777344 | tf_op jit(solution)/shard_map/while/body/eval_jaxpr/jit(_take)/gather | solution.py:21
  325.8 11.7 %fusion.23 = f32[32,1024,128]{2,1,0:T(8,128)} fusion(bf16[32,1024,128]{2,1,0:T(8,128)(2,1)} %gather_fusion, pred[32]{0:T(512)(128)(4,1)S(1)} %and_bitcast_fusion.2, bf16[6,32,128,128]{3,2,1,0:T(8,128)(2,1)} %get-tuple-element.110, s32[]{:T(128)} %get-tuple-element.101), kind=kOutput, calls=%fused_computation.4.clone.1 | convolution fusion | flops 1077936128 | bytes 26214944 | tf_op jit(solution)/shard_map/while/body/eval_jaxpr/rna,nab->rnb/dot_general | solution.py:22
  337.5 21.0 %scatter_fusion = f32[1024,2,128]{2,0,1:T(8,128)S(1)} fusion(f32[1024,2,128]{2,0,1:T(8,128)S(1)} %get-tuple-element.102, s32[32]{0:T(128)S(1)} %get-tuple-element.93, f32[32,1024,128]{2,1,0:T(8,128)} %fusion.23), kind=kCustom, calls=%fused_computation.1.clone.1 | custom fusion | flops 4194304 | bytes 50331776 | tf_op jit(solution)/shard_map/while/body/eval_jaxpr/scatter-add | solution.py:23
  358.6 10.7 %gather_fusion = bf16[32,1024,128]{2,1,0:T(8,128)(2,1)} fusion(bf16[1024,64,128]{2,0,1:T(8,128)(2,1)} %get-tuple-element.111, s32[1024]{0:T(1024)S(1)} %pad_clamp_fusion.2), kind=kCustom, calls=%fused_computation.clone.1 | custom fusion | bytes 16777344 | tf_op jit(solution)/shard_map/while/body/eval_jaxpr/jit(_take)/gather | solution.py:21
  369.2 11.7 %fusion.23 = f32[32,1024,128]{2,1,0:T(8,128)} fusion(bf16[32,1024,128]{2,1,0:T(8,128)(2,1)} %gather_fusion, pred[32]{0:T(512)(128)(4,1)S(1)} %and_bitcast_fusion.2, bf16[6,32,128,128]{3,2,1,0:T(8,128)(2,1)} %get-tuple-element.110, s32[]{:T(128)} %get-tuple-element.101), kind=kOutput, calls=%fused_computation.4.clone.1 | convolution fusion | flops 1077936128 | bytes 26214944 | tf_op jit(solution)/shard_map/while/body/eval_jaxpr/rna,nab->rnb/dot_general | solution.py:22
  381.0 21.0 %scatter_fusion = f32[1024,2,128]{2,0,1:T(8,128)S(1)} fusion(f32[1024,2,128]{2,0,1:T(8,128)S(1)} %get-tuple-element.102, s32[32]{0:T(128)S(1)} %get-tuple-element.93, f32[32,1024,128]{2,1,0:T(8,128)} %fusion.23), kind=kCustom, calls=%fused_computation.1.clone.1 | custom fusion | flops 4194304 | bytes 50331776 | tf_op jit(solution)/shard_map/while/body/eval_jaxpr/scatter-add | solution.py:23
  412.7 11.7 %fusion.23 = f32[32,1024,128]{2,1,0:T(8,128)} fusion(bf16[32,1024,128]{2,1,0:T(8,128)(2,1)} %gather_fusion, pred[32]{0:T(512)(128)(4,1)S(1)} %and_bitcast_fusion.2, bf16[6,32,128,128]{3,2,1,0:T(8,128)(2,1)} %get-tuple-element.110, s32[]{:T(128)} %get-tuple-element.101), kind=kOutput, calls=%fused_computation.4.clone.1 | convolution fusion | flops 1077936128 | bytes 26214944 | tf_op jit(solution)/shard_map/while/body/eval_jaxpr/rna,nab->rnb/dot_general | solution.py:22
  424.4 21.0 %scatter_fusion = f32[1024,2,128]{2,0,1:T(8,128)S(1)} fusion(f32[1024,2,128]{2,0,1:T(8,128)S(1)} %get-tuple-element.102, s32[32]{0:T(128)S(1)} %get-tuple-element.93, f32[32,1024,128]{2,1,0:T(8,128)} %fusion.23), kind=kCustom, calls=%fused_computation.1.clone.1 | custom fusion | flops 4194304 | bytes 50331776 | tf_op jit(solution)/shard_map/while/body/eval_jaxpr/scatter-add | solution.py:23
  445.5 33.0 %all-reduce.1 = bf16[1024,256]{1,0:T(8,128)(2,1)S(1)} all-reduce(f32[1024,256]{1,0:T(8,128)S(1)} %copy_bitcast_fusion), channel_id=1, replica_groups=mesh['pair'=64,'cuts'=4] {'cuts'}, use_global_device_ids=true, to_apply=%region_7.8 | all-reduce | flops 262144 | bytes 1572864 | tf_op jit(solution)/shard_map/psum | solution.py:57
  (45 shorter events, 31.4 us)
Async XLA Ops:
  0.0 21.0 %copy-start = (bf16[96,128,128]{2,1,0:T(8,128)(2,1)S(1)}, bf16[96,128,128]{2,1,0:T(8,128)(2,1)}, u32[]{:S(2)}) copy-start(bf16[96,128,128]{2,1,0:T(8,128)(2,1)} %param.7) | copy-start | bytes 9437188
  5.1 28.6 %all-to-all-start = ((s32[64,3,2]{1,2,0:T(2,128)}), s32[64,3,2]{1,2,0:T(2,128)S(1)}, u32[]{:S(2)}, u32[]{:S(2)}) async-start(s32[64,3,2]{1,2,0:T(2,128)} %copy.20), calls=%async_computation | async-start | bytes 131072 | tf_op jit(solution)/shard_map/all_to_all | solution.py:54
  33.7 151.2 %all-to-all-start.1 = ((bf16[192,128,128]{2,1,0:T(8,128)(2,1)}), bf16[192,128,128]{2,1,0:T(8,128)(2,1)}, u32[]{:S(2)}, u32[]{:S(2)}) async-start(bf16[192,128,128]{2,1,0:T(8,128)(2,1)} %scatter_fusion.1), calls=%async_computation.1 | async-start | bytes 12582912 | tf_op jit(solution)/shard_map/all_to_all | solution.py:53
where the time goes:
time: 484 us; the launch traced here: 479 us
  other arithmetic  129 us (27%)
  local copies, waits for them, and re-layouts  128 us (26%)
  waiting for transfers between devices  95.7 us (20%)
  matrix products  70.3 us (15%)
  blocking collectives  33 us (7%)
  starting transfers between devices  22.2 us (5%)
    scatter-add x6, other arithmetic, one_block(): running = running.at[:, id_block[:, 1], :].add(product)  126 us
    all_to_all x1, waiting for transfers between devices, local(): lax.all_to_all(send_tiles, 'pair', split_axis=0, concat_axis=0, tiled=True)  95.7 us
    dot_general x6, matrix products, one_block(): jnp.einsum('rna,nab->rnb', picked, tile_block, preferred_element_type=jnp...  70.3 us
    gather x6, local copies, waits for them, and re-layouts, one_block(): picked = jnp.take(w_blocks, id_block[:, 0], axis=1)  64 us
    psum x1, blocking collectives, local(): summed = lax.psum(partial_sum, 'cuts')  33 us
    unnamed x3, local copies, waits for them, and re-layouts  22.4 us
    while x1, local copies, waits for them, and re-layouts, contract(): total, _ = lax.scan(one_block, start_value, (grouped_tiles, grouped_ids))  22.4 us
    scatter x1, local copies, waits for them, and re-layouts, local(): jnp.zeros((slot_total, tile_size, tile_size), t2_tiles.dtype).at[slot_index]  12.7 us
  transfers between devices with their start and end apart: 2, of which 1 were waited for; matrix products, arithmetic and copies ran while one was open for 13% of the time, Pallas kernels for 0%

commit v1 on v0

v1 whole, which is shorter than its diff:
```python
import functools

import jax
import jax.numpy as jnp
from jax import lax
from jax.experimental import pallas as pl
from jax.experimental.pallas import tpu as pltpu
from jax.sharding import Mesh
from jax.sharding import PartitionSpec as P

Z, Y, K, X = 8, 4, 2, 4
GROUP = Y * K
CAP = 3
TILE = 128
STEPS = 2
CHUNKS = Z // STEPS
SLOTS = STEPS * CAP
META = 16
BLOCK = SLOTS * TILE + META
DEPTH = 8


def route_kernel(place, kc, jb, owner, tiles, *rest):
    sends = rest[:CHUNKS]
    counts, codes, metas, sem, meta_sem = rest[CHUNKS:]
    held = tiles.shape[0]
    z = place[0]

    def clear(o, carry):
        counts[o] = 0
        return carry

    lax.fori_loop(0, Z * GROUP, clear, 0)
    codes[...] = jnp.full(codes.shape, -1.0, jnp.float32)
    lane = lax.broadcasted_iota(jnp.int32, (1, TILE), 1)

    def one(i, carry):
        o = owner[i]
        rank = counts[o]
        counts[o] = rank + 1
        dest = lax.rem(o, GROUP)
        step = lax.rem(z - 1 - lax.div(o, GROUP) + 2 * Z, Z)
        chunk = lax.div(step, STEPS)
        slot = lax.rem(step, STEPS) * CAP + rank
        row = pl.multiple_of(dest * BLOCK + slot * TILE, 16)
        for c in range(CHUNKS):

            @pl.when(chunk == c)
            def _():
                pltpu.make_async_copy(tiles.at[i], sends[c].at[pl.ds(row, TILE), :], sem).start()

        line = pl.ds(chunk * GROUP + dest, 1)
        code = (kc[i] * 2 + jb[i]).astype(jnp.float32)
        codes[line, :] = jnp.where(lane == slot, code, codes[line, :])
        return carry

    lax.fori_loop(0, held, one, 0)
    metas[...] = jnp.broadcast_to(codes[...][:, None, :], metas.shape).astype(metas.dtype)
    for c in range(CHUNKS):
        for d in range(GROUP):
            pltpu.make_async_copy(
                metas.at[c * GROUP + d],
                sends[c].at[pl.ds(d * BLOCK + SLOTS * TILE, META), :],
                meta_sem.at[c * GROUP + d],
            ).start()
    for c in range(CHUNKS):
        for d in range(GROUP):
            pltpu.make_async_copy(
                metas.at[c * GROUP + d],
                sends[c].at[pl.ds(d * BLOCK + SLOTS * TILE, META), :],
                meta_sem.at[c * GROUP + d],
            ).wait()
    pltpu.make_async_copy(tiles, tiles, sem).wait()


def route(place, kc, jb, owner, tiles):
    smem = pl.BlockSpec(memory_space=pltpu.SMEM)
    hbm = pl.BlockSpec(memory_space=pl.ANY)
    return pl.pallas_call(
        route_kernel,
        out_shape=[jax.ShapeDtypeStruct((GROUP * BLOCK, TILE), tiles.dtype)] * CHUNKS,
        in_specs=[smem] * 4 + [hbm],
        out_specs=[hbm] * CHUNKS,
        scratch_shapes=[
            pltpu.SMEM((Z * GROUP,), jnp.int32),
            pltpu.VMEM((CHUNKS * GROUP, TILE), jnp.float32),
            pltpu.VMEM((CHUNKS * GROUP, META, TILE), jnp.bfloat16),
            pltpu.SemaphoreType.DMA,
            pltpu.SemaphoreType.DMA((CHUNKS * GROUP,)),
        ],
        compiler_params=pltpu.CompilerParams(vmem_limit_bytes=16 << 20),
        name="route",
    )(place, kc, jb, owner, tiles)


def contract_kernel(place, got, w, *rest):
    outs = rest[: X * STEPS]
    total, held, codes_v, codes, rows, cols, sums, code_sem, w_sem = rest[X * STEPS :]
    row_count = w.shape[0]
    part = row_count // X
    lines = [got[d * BLOCK + SLOTS * TILE : (d + 1) * BLOCK, :][0:1] for d in range(GROUP)]
    codes_v[...] = jnp.concatenate(lines, axis=0).astype(jnp.float32).astype(jnp.int32)
    copy = pltpu.make_async_copy(codes_v, codes, code_sem)
    copy.start()
    copy.wait()
    count = jnp.int32(0)
    for d in range(GROUP):
        for slot in range(SLOTS):
            code = codes[d, slot]
            rows[count] = d * BLOCK + slot * TILE
            cols[count] = lax.shift_right_arithmetic(code, 1)
            sums[count] = (slot // CAP) * 2 + (code & 1)
            count = count + jnp.where(code >= 0, 1, 0)

    def fetch(i, b):
        start = pl.multiple_of(cols[i] * TILE, TILE)
        return pltpu.make_async_copy(w.at[:, pl.ds(start, TILE)], held.at[b], w_sem.at[b])

    for b in range(DEPTH):

        @pl.when(b < count)
        def _():
            fetch(b, b).start()

    total[...] = jnp.zeros_like(total)

    def one(i, carry):
        b = lax.rem(i, DEPTH)
        fetch(i, b).wait()
        tile = got[pl.ds(pl.multiple_of(rows[i], 16), TILE), :]
        total[sums[i]] += jnp.dot(held[b], tile, preferred_element_type=jnp.float32)

        @pl.when(i + DEPTH < count)
        def _():
            fetch(i + DEPTH, b).start()

        return carry

    lax.fori_loop(0, count, one, 0)
    x = place[1]
    for away in range(X):
        first = pl.multiple_of(lax.rem(x + away, X) * part, part)
        for s in range(STEPS):
            for j in range(2):
                outs[away * STEPS + s][:, j * TILE : (j + 1) * TILE] = total[
                    s * 2 + j, pl.ds(first, part), :
                ]


def contract(place, got, w):
    smem = pl.BlockSpec(memory_space=pltpu.SMEM)
    vmem = pl.BlockSpec(memory_space=pltpu.VMEM)
    row_count = w.shape[0]
    most = GROUP * SLOTS
    return pl.pallas_call(
        contract_kernel,
        out_shape=[jax.ShapeDtypeStruct((row_count // X, 2 * TILE), jnp.float32)] * (X * STEPS),
        in_specs=[smem, vmem, pl.BlockSpec(memory_space=pl.ANY)],
        out_specs=[vmem] * (X * STEPS),
        scratch_shapes=[
            pltpu.VMEM((2 * STEPS, row_count, TILE), jnp.float32),
            pltpu.VMEM((DEPTH, row_count, TILE), jnp.bfloat16),
            pltpu.VMEM((GROUP, TILE), jnp.int32),
            pltpu.SMEM((GROUP, TILE), jnp.int32),
            pltpu.SMEM((most + 1,), jnp.int32),
            pltpu.SMEM((most + 1,), jnp.int32),
            pltpu.SMEM((most + 1,), jnp.int32),
            pltpu.SemaphoreType.DMA,
            pltpu.SemaphoreType.DMA((DEPTH,)),
        ],
        compiler_params=pltpu.CompilerParams(vmem_limit_bytes=24 << 20),
        cost_estimate=pl.CostEstimate(
            flops=most * row_count * TILE * TILE, bytes_accessed=16 << 20, transcendentals=0
        ),
        name="contract",
    )(place, got, w)


def local(t2_tiles, kc_tile, jb_tile, tile_owner, w_slices):
    z, x = lax.axis_index("z"), lax.axis_index("x")
    place = jnp.stack([z, x]).astype(jnp.int32)
    up_x = [(i, (i + 1) % X) for i in range(X)]
    down_x = [(i, (i - 1) % X) for i in range(X)]
    up_z = [(i, (i + 1) % Z) for i in range(Z)]
    sends = route(place, kc_tile, jb_tile, tile_owner[:, 0], t2_tiles)
    gots = [lax.all_to_all(s, ("y", "k"), split_axis=0, concat_axis=0, tiled=True) for s in sends]
    running = None
    for c in range(CHUNKS):
        own_a, own_b, next_a, next_b, far_a, far_b, last_a, last_b = contract(
            place, gots[c], w_slices
        )
        from_low_far = lax.ppermute(far_b, "x", up_x)
        from_high_far = lax.ppermute(far_a, "x", down_x)
        from_low_a = lax.ppermute(next_a, "x", up_x)
        from_high_b = lax.ppermute(last_b, "x", down_x)
        from_low_b = lax.ppermute(next_b + from_low_far, "x", up_x)
        from_high_a = lax.ppermute(last_a + from_high_far, "x", down_x)
        first = own_a + from_low_a + from_high_a
        if running is not None:
            first = first + running
        second = own_b + from_low_b + from_high_b + lax.ppermute(first, "z", up_z)
        if c < CHUNKS - 1:
            running = lax.ppermute(second, "z", up_z)
    return second.astype(jnp.bfloat16)


def solution(mesh):
    fine = Mesh(mesh.devices.reshape(Z, Y, K, X), ("z", "y", "k", "x"))
    pair = ("z", "y", "k")
    every = ("z", "y", "k", "x")
    return jax.shard_map(
        local,
        mesh=fine,
        in_specs=(
            P(every, None, None),
            P(every),
            P(every),
            P(every, None),
            P(None, "x"),
        ),
        out_specs=P("x", pair),
        check_vma=False,
    )
```

time: 484 us -> 216 us (0.45)
  the two profiles are of different devices: /device:TPU:32 before, /device:TPU:16 now
where the time goes in v1:
time: 216 us; the launch traced here: 213 us
  starting transfers between devices  52.7 us (24%)
  blocking collectives  49.6 us (23%)
  Pallas kernels  46 us (21%)
  waiting for transfers between devices  31 us (14%)
  local copies, waits for them, and re-layouts  22.6 us (10%)
  other arithmetic  10.4 us (5%)
    all_to_all x2, blocking collectives, local(): lax.all_to_all(s, ('y', 'k'), split_axis=0, concat_axis=0, tiled=True)  49.6 us
    pallas_call x4, Pallas kernels, contract(): pl.pallas_call(contract_kernel, out_shape=[jax.ShapeDtypeStruct((row_coun...  36.7 us
    unnamed x50, local copies, waits for them, and re-layouts  22.6 us
    all_to_all x2, starting transfers between devices, local(): lax.all_to_all(s, ('y', 'k'), split_axis=0, concat_axis=0, tiled=True)  15.9 us
    ppermute x4, starting transfers between devices, local(): from_high_a = lax.ppermute(last_a + from_high_far, 'x', down_x)  11.4 us
    ppermute x4, waiting for transfers between devices, local(): from_high_far = lax.ppermute(far_a, 'x', down_x)  10.3 us
    pallas_call x1, Pallas kernels, route(): pl.pallas_call(route_kernel, out_shape=[jax.ShapeDtypeStruct((GROUP * BLO...  9.32 us
    ppermute x4, waiting for transfers between devices, local(): second = own_b + from_low_b + from_high_b + lax.ppermute(first, 'z', up_z)  6.69 us
  transfers between devices with their start and end apart: 33, of which 9 were waited for; matrix products, arithmetic and copies ran while one was open for 5% of the time, Pallas kernels for 17%

profile of v1, /device:TPU:16, one launch (start us, length us, event | category | flops | bytes accessed | tf_op | source)
XLA Modules:
  0.0 212.6 jit_solution(14884549715014722985)
XLA Ops:
  3.9 9.3 %route.1 = (bf16[6272,128]{1,0:T(8,128)(2,1)S(1)}, bf16[6272,128]{1,0:T(8,128)(2,1)S(1)}, bf16[6272,128]{1,0:T(8,128)(2,1)S(1)}, bf16[6272,128]{1,0:T(8,128)(2,1)S(1)}) custom-call(s32[2]{0:T(128)S(1)} %pad_add_fusion.place, s32[96]{0:T(128)S(1)} %copy-done.19, s32[96]{0:T(128)S(1)} %copy-done.20, s32[96]{0:T(128)S(1)} %bitcast.19, ...), custom_call_target="tpu_custom_call" | custom-call | tf_op jit(solution)/shard_map/route/pallas_call | solution.py:79
  13.3 24.3 %all_to_all.44 = bf16[8,784,128]{2,1,0:T(8,128)(2,1)S(1)} all-to-all(bf16[8,784,128]{2,1,0:T(8,128)(2,1)S(1)} %bitcast.18), channel_id=1, replica_groups=mesh['z'=8,'y'=4,'k'=2,'x'=4] {'y','k'}, dimensions={0} | all-to-all | bytes 3211264 | tf_op jit(solution)/shard_map/all_to_all | solution.py:186
  37.6 25.3 %all_to_all.45 = bf16[8,784,128]{2,1,0:T(8,128)(2,1)} all-to-all(bf16[8,784,128]{2,1,0:T(8,128)(2,1)S(1)} %bitcast.17), channel_id=1, replica_groups=mesh['z'=8,'y'=4,'k'=2,'x'=4] {'y','k'}, dimensions={0} | all-to-all | bytes 3211264 | tf_op jit(solution)/shard_map/all_to_all | solution.py:186
  62.9 5.9 %all-to-all-start.1 = ((bf16[8,784,128]{2,1,0:T(8,128)(2,1)}), bf16[8,784,128]{2,1,0:T(8,128)(2,1)S(1)}, u32[]{:S(2)}, u32[]{:S(2)}) async-start(bf16[8,784,128]{2,1,0:T(8,128)(2,1)} %bitcast.16), calls=%async_computation.1 | async-start | bytes 3211264 | tf_op jit(solution)/shard_map/all_to_all | solution.py:186
  68.8 5.8 %copy-done = bf16[1024,8192]{1,0:T(8,128)(2,1)S(1)} copy-done((bf16[1024,8192]{1,0:T(8,128)(2,1)S(1)}, bf16[1024,8192]{1,0:T(8,128)(2,1)}, u32[]{:S(2)}) %copy-start) | copy-done | bytes 16777240
  76.0 7.1 %contract.7 = (f32[256,256]{1,0:T(8,128)S(1)}, f32[256,256]{1,0:T(8,128)S(1)}, f32[256,256]{1,0:T(8,128)S(1)}, f32[256,256]{1,0:T(8,128)S(1)}, f32[256,256]{1,0:...) custom-call(s32[2]{0:T(128)S(1)} %pad_add_fusion.place, ...), custom_call_target="tpu_custom_call" | custom-call | flops 805306368 | bytes 16777216 | tf_op jit(solution)/shard_map/contract/pallas_call | solution.py:155
  83.1 2.8 %collective-permute-start.22 = (f32[256,256]{1,0:T(8,128)S(1)}, f32[256,256]{1,0:T(8,128)S(1)}, u32[]{:S(2)}, u32[]{:S(2)}) collective-permute-start(f32[256,256]{1,0:T(8,128)S(1)} %get-tuple-element.76), channel_id=1, source_target_pairs={{0,3},{1,0},{2,1},{3,2},{4,7},{5,4},{6,5},{7,6},{8,11},{9,8},{10,9... | collective-permute-start | bytes 786440 | tf_op jit(solution)/shard_map/ppermute | solution.py:193
  86.7 5.1 %collective-permute-done.22 = f32[256,256]{1,0:T(8,128)S(1)} collective-permute-done((f32[256,256]{1,0:T(8,128)S(1)}, f32[256,256]{1,0:T(8,128)S(1)}, u32[]{:S(2)}, u32[]{:S(2)}) %collective-permute-start.22) | collective-permute-done | bytes 262176 | tf_op jit(solution)/shard_map/ppermute | solution.py:193
  91.9 3.8 %collective-permute-start.23 = (f32[256,256]{1,0:T(8,128)S(1)}, f32[256,256]{1,0:T(8,128)S(1)}, u32[]{:S(2)}, u32[]{:S(2)}) collective-permute-start(f32[256,256]{1,0:T(8,128)S(1)} %add.115), channel_id=1, source_target_pairs={{0,3},{1,0},{2,1},{3,2},{4,7},{5,4},{6,5},{7,6},{8,11},{9,8},{10,9... | collective-permute-start | bytes 786440 | tf_op jit(solution)/shard_map/ppermute | solution.py:197
  95.7 9.4 %contract.6 = (f32[256,256]{1,0:T(8,128)S(1)}, f32[256,256]{1,0:T(8,128)S(1)}, f32[256,256]{1,0:T(8,128)}, f32[256,256]{1,0:T(8,128)S(1)}, f32[256,256]{1,0:T(8,...) custom-call(s32[2]{0:T(128)S(1)} %pad_add_fusion.place, ...), custom_call_target="tpu_custom_call" | custom-call | flops 805306368 | bytes 16777216 | tf_op jit(solution)/shard_map/contract/pallas_call | solution.py:155
  108.8 2.2 %collective-permute-start.24 = (f32[256,256]{1,0:T(8,128)}, f32[256,256]{1,0:T(8,128)}, u32[]{:S(2)}, u32[]{:S(2)}) collective-permute-start(f32[256,256]{1,0:T(8,128)} %add_add_fusion), channel_id=1, source_target_pairs={{0,32},{32,64},{64,96},{96,128},{128,160},{160,192},{192,224},{224... | collective-permute-start | bytes 786440 | tf_op jit(solution)/shard_map/ppermute | solution.py:201
  115.2 9.9 %all-to-all-start = ((bf16[8,784,128]{2,1,0:T(8,128)(2,1)}), bf16[8,784,128]{2,1,0:T(8,128)(2,1)S(1)}, u32[]{:S(2)}, u32[]{:S(2)}) async-start(bf16[8,784,128]{2,1,0:T(8,128)(2,1)} %bitcast.15), calls=%async_computation | async-start | bytes 3211264 | tf_op jit(solution)/shard_map/all_to_all | solution.py:186
  125.1 3.2 %collective-permute-start.17 = (f32[256,256]{1,0:T(8,128)}, f32[256,256]{1,0:T(8,128)S(1)}, u32[]{:S(2)}, u32[]{:S(2)}) collective-permute-start(f32[256,256]{1,0:T(8,128)} %add.109), channel_id=1, source_target_pairs={{0,3},{1,0},{2,1},{3,2},{4,7},{5,4},{6,5},{7,6},{8,11},{9,8},{10,9... | collective-permute-start | bytes 786440 | tf_op jit(solution)/shard_map/ppermute | solution.py:197
  132.0 5.8 %copy-done.2 = bf16[1024,8192]{1,0:T(8,128)(2,1)S(1)} copy-done((bf16[1024,8192]{1,0:T(8,128)(2,1)S(1)}, bf16[1024,8192]{1,0:T(8,128)(2,1)}, u32[]{:S(2)}) %copy-start.2) | copy-done | bytes 16777240
  137.7 9.3 %contract.5 = (f32[256,256]{1,0:T(8,128)S(1)}, f32[256,256]{1,0:T(8,128)S(1)}, f32[256,256]{1,0:T(8,128)}, f32[256,256]{1,0:T(8,128)S(1)}, f32[256,256]{1,0:T(8,...) custom-call(s32[2]{0:T(128)S(1)} %pad_add_fusion.place, ...), custom_call_target="tpu_custom_call" | custom-call | flops 805306368 | bytes 16777216 | tf_op jit(solution)/shard_map/contract/pallas_call | solution.py:155
  153.0 2.8 %collective-permute-done.10 = f32[256,256]{1,0:T(8,128)S(1)} collective-permute-done((f32[256,256]{1,0:T(8,128)S(1)}, f32[256,256]{1,0:T(8,128)S(1)}, u32[]{:S(2)}, u32[]{:S(2)}) %collective-permute-start.10) | collective-permute-done | bytes 262176 | tf_op jit(solution)/shard_map/ppermute | solution.py:193
  157.5 2.3 %collective-permute-start.11 = (f32[256,256]{1,0:T(8,128)}, f32[256,256]{1,0:T(8,128)}, u32[]{:S(2)}, u32[]{:S(2)}) collective-permute-start(f32[256,256]{1,0:T(8,128)} %add.103), channel_id=1, source_target_pairs={{0,3},{1,0},{2,1},{3,2},{4,7},{5,4},{6,5},{7,6},{8,11},{9,8},{10,9... | collective-permute-start | bytes 786440 | tf_op jit(solution)/shard_map/ppermute | solution.py:197
  162.6 5.8 %copy-done.3 = bf16[1024,8192]{1,0:T(8,128)(2,1)S(1)} copy-done((bf16[1024,8192]{1,0:T(8,128)(2,1)S(1)}, bf16[1024,8192]{1,0:T(8,128)(2,1)}, u32[]{:S(2)}) %copy-start.3) | copy-done | bytes 16777240
  168.4 10.8 %contract.4 = (f32[256,256]{1,0:T(8,128)S(1)}, f32[256,256]{1,0:T(8,128)S(1)}, f32[256,256]{1,0:T(8,128)S(1)}, f32[256,256]{1,0:T(8,128)S(1)}, f32[256,256]{1,0:...) custom-call(s32[2]{0:T(128)S(1)} %pad_add_fusion.place, ...), custom_call_target="tpu_custom_call" | custom-call | flops 805306368 | bytes 16777216 | tf_op jit(solution)/shard_map/contract/pallas_call | solution.py:155
  186.1 2.3 %collective-permute-done.4 = f32[256,256]{1,0:T(8,128)S(1)} collective-permute-done((f32[256,256]{1,0:T(8,128)S(1)}, f32[256,256]{1,0:T(8,128)S(1)}, u32[]{:S(2)}, u32[]{:S(2)}) %collective-permute-start.4) | collective-permute-done | bytes 262176 | tf_op jit(solution)/shard_map/ppermute | solution.py:193
  195.0 3.5 %collective-permute-done = f32[256,256]{1,0:T(8,128)S(1)} collective-permute-done((f32[256,256]{1,0:T(8,128)S(1)}, f32[256,256]{1,0:T(8,128)S(1)}, u32[]{:S(2)}, u32[]{:S(2)}) %collective-permute-start) | collective-permute-done | bytes 262176 | tf_op jit(solution)/shard_map/ppermute | solution.py:192
  198.7 5.5 %collective-permute-done.3 = f32[256,256]{1,0:T(8,128)S(1)} collective-permute-done((f32[256,256]{1,0:T(8,128)S(1)}, f32[256,256]{1,0:T(8,128)S(1)}, u32[]{:S(2)}, u32[]{:S(2)}) %collective-permute-start.3) | collective-permute-done | bytes 262176 | tf_op jit(solution)/shard_map/ppermute | solution.py:194
  204.3 2.8 %collective-permute-done.1 = f32[256,256]{1,0:T(8,128)S(1)} collective-permute-done((f32[256,256]{1,0:T(8,128)S(1)}, f32[256,256]{1,0:T(8,128)S(1)}, u32[]{:S(2)}, u32[]{:S(2)}) %collective-permute-start.1) | collective-permute-done | bytes 262176 | tf_op jit(solution)/shard_map/ppermute | solution.py:196
  207.1 4.8 %collective-permute-done.30 = f32[256,256]{1,0:T(8,128)S(1)} collective-permute-done((f32[256,256]{1,0:T(8,128)S(1)}, f32[256,256]{1,0:T(8,128)S(1)}, u32[]{:S(2)}, u32[]{:S(2)}) %collective-permute-start.30) | collective-permute-done | bytes 262176 | tf_op jit(solution)/shard_map/ppermute | solution.py:201
  (116 shorter events, 42.4 us)
Async XLA Ops:
  62.9 52.3 %all-to-all-start.1 = ((bf16[8,784,128]{2,1,0:T(8,128)(2,1)}), bf16[8,784,128]{2,1,0:T(8,128)(2,1)S(1)}, u32[]{:S(2)}, u32[]{:S(2)}) async-start(bf16[8,784,128]{2,1,0:T(8,128)(2,1)} %bitcast.16), calls=%async_computation.1 | async-start | bytes 3211264 | tf_op jit(solution)/shard_map/all_to_all | solution.py:186
  85.9 19.7 %collective-permute-start.18 = (f32[256,256]{1,0:T(8,128)S(1)}, f32[256,256]{1,0:T(8,128)S(1)}, u32[]{:S(2)}, u32[]{:S(2)}) collective-permute-start(f32[256,256]{1,0:T(8,128)S(1)} %get-tuple-element.71), channel_id=1, source_target_pairs={{0,1},{1,2},{2,3},{3,0},{4,5},{5,6},{6,7},{7,4},{8,9},{9,10},{10,1... | collective-permute-start | bytes 786440 | tf_op jit(solution)/shard_map/ppermute | solution.py:192
  85.9 22.1 %collective-permute-start.21 = (f32[256,256]{1,0:T(8,128)S(1)}, f32[256,256]{1,0:T(8,128)S(1)}, u32[]{:S(2)}, u32[]{:S(2)}) collective-permute-start(f32[256,256]{1,0:T(8,128)S(1)} %get-tuple-element.74), channel_id=1, source_target_pairs={{0,1},{1,2},{2,3},{3,0},{4,5},{5,6},{6,7},{7,4},{8,9},{9,10},{10,1... | collective-permute-start | bytes 786440 | tf_op jit(solution)/shard_map/ppermute | solution.py:194
  91.9 16.2 %collective-permute-start.23 = (f32[256,256]{1,0:T(8,128)S(1)}, f32[256,256]{1,0:T(8,128)S(1)}, u32[]{:S(2)}, u32[]{:S(2)}) collective-permute-start(f32[256,256]{1,0:T(8,128)S(1)} %add.115), channel_id=1, source_target_pairs={{0,3},{1,0},{2,1},{3,2},{4,7},{5,4},{6,5},{7,6},{8,11},{9,8},{10,9... | collective-permute-start | bytes 786440 | tf_op jit(solution)/shard_map/ppermute | solution.py:197
  95.6 29.5 %collective-permute-start.20 = (f32[256,256]{1,0:T(8,128)}, f32[256,256]{1,0:T(8,128)}, u32[]{:S(2)}, u32[]{:S(2)}) collective-permute-start(f32[256,256]{1,0:T(8,128)} %get-tuple-element.72), channel_id=1, source_target_pairs={{0,3},{1,0},{2,1},{3,2},{4,7},{5,4},{6,5},{7,6},{8,11},{9,8},{10,9... | collective-permute-start | bytes 786440 | tf_op jit(solution)/shard_map/ppermute | solution.py:195
  106.3 22.0 %collective-permute-start.19 = (f32[256,256]{1,0:T(8,128)}, f32[256,256]{1,0:T(8,128)}, u32[]{:S(2)}, u32[]{:S(2)}) collective-permute-start(f32[256,256]{1,0:T(8,128)} %add.111), channel_id=1, source_target_pairs={{0,1},{1,2},{2,3},{3,0},{4,5},{5,6},{6,7},{7,4},{8,9},{9,10},{10,1... | collective-permute-start | bytes 786440 | tf_op jit(solution)/shard_map/ppermute | solution.py:196
  108.8 19.5 %collective-permute-start.24 = (f32[256,256]{1,0:T(8,128)}, f32[256,256]{1,0:T(8,128)}, u32[]{:S(2)}, u32[]{:S(2)}) collective-permute-start(f32[256,256]{1,0:T(8,128)} %add_add_fusion), channel_id=1, source_target_pairs={{0,32},{32,64},{64,96},{96,128},{128,160},{160,192},{192,224},{224... | collective-permute-start | bytes 786440 | tf_op jit(solution)/shard_map/ppermute | solution.py:201
  111.0 36.1 %collective-permute-start.12 = (f32[256,256]{1,0:T(8,128)}, f32[256,256]{1,0:T(8,128)}, u32[]{:S(2)}, u32[]{:S(2)}) collective-permute-start(f32[256,256]{1,0:T(8,128)} %get-tuple-element.62), channel_id=1, source_target_pairs={{0,1},{1,2},{2,3},{3,0},{4,5},{5,6},{6,7},{7,4},{8,9},{9,10},{10,1... | collective-permute-start | bytes 786440 | tf_op jit(solution)/shard_map/ppermute | solution.py:192
  112.9 35.5 %collective-permute-start.15 = (f32[256,256]{1,0:T(8,128)}, f32[256,256]{1,0:T(8,128)}, u32[]{:S(2)}, u32[]{:S(2)}) collective-permute-start(f32[256,256]{1,0:T(8,128)} %get-tuple-element.65), channel_id=1, source_target_pairs={{0,1},{1,2},{2,3},{3,0},{4,5},{5,6},{6,7},{7,4},{8,9},{9,10},{10,1... | collective-permute-start | bytes 786440 | tf_op jit(solution)/shard_map/ppermute | solution.py:194
  115.2 47.4 %all-to-all-start = ((bf16[8,784,128]{2,1,0:T(8,128)(2,1)}), bf16[8,784,128]{2,1,0:T(8,128)(2,1)S(1)}, u32[]{:S(2)}, u32[]{:S(2)}) async-start(bf16[8,784,128]{2,1,0:T(8,128)(2,1)} %bitcast.15), calls=%async_computation | async-start | bytes 3211264 | tf_op jit(solution)/shard_map/all_to_all | solution.py:186
  125.1 25.2 %collective-permute-start.17 = (f32[256,256]{1,0:T(8,128)}, f32[256,256]{1,0:T(8,128)S(1)}, u32[]{:S(2)}, u32[]{:S(2)}) collective-permute-start(f32[256,256]{1,0:T(8,128)} %add.109), channel_id=1, source_target_pairs={{0,3},{1,0},{2,1},{3,2},{4,7},{5,4},{6,5},{7,6},{8,11},{9,8},{10,9... | collective-permute-start | bytes 786440 | tf_op jit(solution)/shard_map/ppermute | solution.py:197
  129.6 20.7 %collective-permute-start.25 = (f32[256,256]{1,0:T(8,128)S(1)}, f32[256,256]{1,0:T(8,128)S(1)}, u32[]{:S(2)}, u32[]{:S(2)}) collective-permute-start(f32[256,256]{1,0:T(8,128)S(1)} %add_add_fusion.1), channel_id=1, source_target_pairs={{0,32},{32,64},{64,96},{96,128},{128,160},{160,192},{192,224},{224... | collective-permute-start | bytes 786440 | tf_op jit(solution)/shard_map/ppermute | solution.py:203
  130.7 26.8 %collective-permute-start.14 = (f32[256,256]{1,0:T(8,128)}, f32[256,256]{1,0:T(8,128)S(1)}, u32[]{:S(2)}, u32[]{:S(2)}) collective-permute-start(f32[256,256]{1,0:T(8,128)} %copy-done.22), channel_id=1, source_target_pairs={{0,3},{1,0},{2,1},{3,2},{4,7},{5,4},{6,5},{7,6},{8,11},{9,8},{10,9... | collective-permute-start | bytes 786440 | tf_op jit(solution)/shard_map/ppermute | solution.py:195
  148.5 11.3 %collective-permute-start.13 = (f32[256,256]{1,0:T(8,128)S(1)}, f32[256,256]{1,0:T(8,128)S(1)}, u32[]{:S(2)}, u32[]{:S(2)}) collective-permute-start(f32[256,256]{1,0:T(8,128)S(1)} %add.105), channel_id=1, source_target_pairs={{0,1},{1,2},{2,3},{3,0},{4,5},{5,6},{6,7},{7,4},{8,9},{9,10},{10,1... | collective-permute-start | bytes 786440 | tf_op jit(solution)/shard_map/ppermute | solution.py:196
  151.5 29.1 %collective-permute-start.6 = (f32[256,256]{1,0:T(8,128)}, f32[256,256]{1,0:T(8,128)}, u32[]{:S(2)}, u32[]{:S(2)}) collective-permute-start(f32[256,256]{1,0:T(8,128)} %get-tuple-element.53), channel_id=1, source_target_pairs={{0,1},{1,2},{2,3},{3,0},{4,5},{5,6},{6,7},{7,4},{8,9},{9,10},{10,1... | collective-permute-start | bytes 786440 | tf_op jit(solution)/shard_map/ppermute | solution.py:192
  155.8 26.6 %collective-permute-start.9 = (f32[256,256]{1,0:T(8,128)}, f32[256,256]{1,0:T(8,128)}, u32[]{:S(2)}, u32[]{:S(2)}) collective-permute-start(f32[256,256]{1,0:T(8,128)} %get-tuple-element.56), channel_id=1, source_target_pairs={{0,1},{1,2},{2,3},{3,0},{4,5},{5,6},{6,7},{7,4},{8,9},{9,10},{10,1... | collective-permute-start | bytes 786440 | tf_op jit(solution)/shard_map/ppermute | solution.py:194
  157.5 26.5 %collective-permute-start.11 = (f32[256,256]{1,0:T(8,128)}, f32[256,256]{1,0:T(8,128)}, u32[]{:S(2)}, u32[]{:S(2)}) collective-permute-start(f32[256,256]{1,0:T(8,128)} %add.103), channel_id=1, source_target_pairs={{0,3},{1,0},{2,1},{3,2},{4,7},{5,4},{6,5},{7,6},{8,11},{9,8},{10,9... | collective-permute-start | bytes 786440 | tf_op jit(solution)/shard_map/ppermute | solution.py:197
  162.5 21.4 %collective-permute-start.27 = (f32[256,256]{1,0:T(8,128)}, f32[256,256]{1,0:T(8,128)}, u32[]{:S(2)}, u32[]{:S(2)}) collective-permute-start(f32[256,256]{1,0:T(8,128)} %add_add_fusion.3), channel_id=1, source_target_pairs={{0,32},{32,64},{64,96},{96,128},{128,160},{160,192},{192,224},{224... | collective-permute-start | bytes 786440 | tf_op jit(solution)/shard_map/ppermute | solution.py:203
  180.6 10.8 %collective-permute-start.8 = (f32[256,256]{1,0:T(8,128)S(1)}, f32[256,256]{1,0:T(8,128)S(1)}, u32[]{:S(2)}, u32[]{:S(2)}) collective-permute-start(f32[256,256]{1,0:T(8,128)S(1)} %copy-done.24), channel_id=1, source_target_pairs={{0,3},{1,0},{2,1},{3,2},{4,7},{5,4},{6,5},{7,6},{8,11},{9,8},{10,9... | collective-permute-start | bytes 786440 | tf_op jit(solution)/shard_map/ppermute | solution.py:195
  182.4 11.1 %collective-permute-start.7 = (f32[256,256]{1,0:T(8,128)S(1)}, f32[256,256]{1,0:T(8,128)S(1)}, u32[]{:S(2)}, u32[]{:S(2)}) collective-permute-start(f32[256,256]{1,0:T(8,128)S(1)} %add.99), channel_id=1, source_target_pairs={{0,1},{1,2},{2,3},{3,0},{4,5},{5,6},{6,7},{7,4},{8,9},{9,10},{10,1... | collective-permute-start | bytes 786440 | tf_op jit(solution)/shard_map/ppermute | solution.py:196
  185.2 13.3 %collective-permute-start = (f32[256,256]{1,0:T(8,128)S(1)}, f32[256,256]{1,0:T(8,128)S(1)}, u32[]{:S(2)}, u32[]{:S(2)}) collective-permute-start(f32[256,256]{1,0:T(8,128)S(1)} %get-tuple-element.44), channel_id=1, source_target_pairs={{0,1},{1,2},{2,3},{3,0},{4,5},{5,6},{6,7},{7,4},{8,9},{9,10},{10,1... | collective-permute-start | bytes 786440 | tf_op jit(solution)/shard_map/ppermute | solution.py:192
  188.4 15.7 %collective-permute-start.3 = (f32[256,256]{1,0:T(8,128)S(1)}, f32[256,256]{1,0:T(8,128)S(1)}, u32[]{:S(2)}, u32[]{:S(2)}) collective-permute-start(f32[256,256]{1,0:T(8,128)S(1)} %get-tuple-element.47), channel_id=1, source_target_pairs={{0,1},{1,2},{2,3},{3,0},{4,5},{5,6},{6,7},{7,4},{8,9},{9,10},{10,1... | collective-permute-start | bytes 786440 | tf_op jit(solution)/shard_map/ppermute | solution.py:194
  191.4 12.7 %collective-permute-start.5 = (f32[256,256]{1,0:T(8,128)S(1)}, f32[256,256]{1,0:T(8,128)S(1)}, u32[]{:S(2)}, u32[]{:S(2)}) collective-permute-start(f32[256,256]{1,0:T(8,128)S(1)} %add.97), channel_id=1, source_target_pairs={{0,3},{1,0},{2,1},{3,2},{4,7},{5,4},{6,5},{7,6},{8,11},{9,8},{10,9... | collective-permute-start | bytes 786440 | tf_op jit(solution)/shard_map/ppermute | solution.py:197
  193.7 10.6 %collective-permute-start.2 = (f32[256,256]{1,0:T(8,128)S(1)}, f32[256,256]{1,0:T(8,128)S(1)}, u32[]{:S(2)}, u32[]{:S(2)}) collective-permute-start(f32[256,256]{1,0:T(8,128)S(1)} %get-tuple-element.45), channel_id=1, source_target_pairs={{0,3},{1,0},{2,1},{3,2},{4,7},{5,4},{6,5},{7,6},{8,11},{9,8},{10,9... | collective-permute-start | bytes 786440 | tf_op jit(solution)/shard_map/ppermute | solution.py:195
  (34 other events, 359.5 us)

commit v2 on v0

v2 whole, which is shorter than its diff:
```python
import jax
import jax.numpy as jnp
from jax import lax
from jax.experimental import pallas as pl
from jax.experimental.pallas import tpu as pltpu
from jax.sharding import Mesh
from jax.sharding import PartitionSpec as P

HIGH, LOW, Y, K, X = 4, 2, 4, 2, 4
GROUP = LOW * Y * K
CAP = 3
TILE = 128
META = 16
DEPTH = 4
WIDE = 4
ORDER = (2, 1, 3, 0)
CHUNKS = (4,)
FIRST = (0,)
CALLS = ((0, 0, 2), (0, 2, 2))


def slots_of(steps):
    return steps * CAP


def block_of(steps):
    return slots_of(steps) * TILE + META


def route_kernel(chunk, kc, jb, owner, tiles, send, *scratch):
    kc_s, jb_s, owner_s, counts, codes, kind_sem, sem = scratch
    held = tiles.shape[0]
    steps = CHUNKS[chunk]
    loads = [
        pltpu.make_async_copy(a, b, kind_sem.at[i])
        for i, (a, b) in enumerate(((kc, kc_s), (jb, jb_s), (owner, owner_s)))
    ]
    for load in loads:
        load.start()

    def clear(o, carry):
        counts[o] = 0
        return carry

    lax.fori_loop(0, HIGH * GROUP, clear, 0)
    codes[...] = jnp.full(codes.shape, -1.0, jnp.float32)
    lane = lax.broadcasted_iota(jnp.int32, (1, TILE), 1)
    high = lax.axis_index("zh")
    for load in loads:
        load.wait()

    def one(i, sent):
        name = owner_s[i]
        away = (lax.shift_right_logical(name, 4) - high) & (HIGH - 1)
        step = jnp.int32(-1)
        for s in range(steps):
            step = jnp.where(away == ORDER[FIRST[chunk] + s], s, step)

        @pl.when(step >= 0)
        def _():
            rank = counts[name]
            counts[name] = rank + 1
            dest = name & (GROUP - 1)
            slot = step * CAP + rank
            row = pl.multiple_of(slot * TILE, TILE)
            pltpu.make_async_copy(tiles.at[i], send.at[dest, pl.ds(row, TILE), :], sem).start()
            line = pl.ds(dest, 1)
            code = (kc_s[i] * 2 + jb_s[i]).astype(jnp.float32)
            codes[line, :] = jnp.where(lane == slot, code, codes[line, :])

        return sent + jnp.where(step >= 0, 1, 0)

    sent = lax.fori_loop(0, held, one, 0)
    send[:, slots_of(steps) * TILE :, :] = jnp.broadcast_to(
        codes[...][:, None, :], (GROUP, META, TILE)
    ).astype(send.dtype)

    def arrived(i, carry):
        pltpu.make_async_copy(tiles.at[0], send.at[0, pl.ds(0, TILE), :], sem).wait()
        return carry

    lax.fori_loop(0, sent, arrived, 0)


def route(chunk, kc, jb, owner, tiles):
    hbm = pl.BlockSpec(memory_space=pltpu.HBM)
    held = tiles.shape[0]

    def kernel(*refs):
        route_kernel(chunk, *refs)

    return pl.pallas_call(
        kernel,
        out_shape=jax.ShapeDtypeStruct((GROUP, block_of(CHUNKS[chunk]), TILE), tiles.dtype),
        in_specs=[hbm] * 4,
        out_specs=pl.BlockSpec(memory_space=pltpu.VMEM),
        scratch_shapes=[
            pltpu.SMEM((held,), jnp.int32),
            pltpu.SMEM((held,), jnp.int32),
            pltpu.SMEM((held,), jnp.int32),
            pltpu.SMEM((HIGH * GROUP,), jnp.int32),
            pltpu.VMEM((GROUP, TILE), jnp.float32),
            pltpu.SemaphoreType.DMA((3,)),
            pltpu.SemaphoreType.DMA,
        ],
        compiler_params=pltpu.CompilerParams(vmem_limit_bytes=60 << 20),
        cost_estimate=pl.CostEstimate(flops=0, bytes_accessed=8 << 20, transcendentals=0),
        name="route",
    )(kc, jb, owner, tiles)


def contract_kernel(begin, steps, got, w, *rest):
    outs = rest[:6]
    tiles, total, held, codes_b, codes_v, codes, rows, cols, sums, sems, w_sem = rest[6:]
    row_count = w.shape[0]
    half = row_count // X // 2
    slots = slots_of(steps)
    zero = GROUP * slots
    metas = pltpu.make_async_copy(got.at[:, pl.ds(got.shape[1] - META, META), :], codes_b, sems.at[0])
    metas.start()
    arrives = []
    for j in range(GROUP):
        arrives.append(
            pltpu.make_async_copy(
                got.at[j, pl.ds(begin * CAP * TILE, slots * TILE), :],
                tiles.at[pl.ds(j * slots * TILE, slots * TILE), :],
                sems.at[2 + j],
            )
        )
    for arrive in arrives:
        arrive.start()
    tiles[zero * TILE :, :] = jnp.zeros((TILE, TILE), tiles.dtype)
    metas.wait()
    codes_v[...] = codes_b[...][:, 0, :].astype(jnp.float32).astype(jnp.int32)
    copy = pltpu.make_async_copy(codes_v, codes, sems.at[1])
    copy.start()
    total[...] = jnp.zeros_like(total)
    copy.wait()
    count = jnp.int32(0)
    for which in range(2 * steps):
        for j in range(GROUP):
            for rank in range(CAP):
                slot = which // 2 * CAP + rank
                code = codes[j, begin * CAP + slot]
                rows[count] = (j * slots + slot) * TILE
                cols[count] = lax.shift_right_arithmetic(code, 1) * TILE
                sums[count] = which
                count = count + jnp.where((code >= 0) & ((code & 1) == which % 2), 1, 0)
        for _ in range(WIDE - 1):
            rows[count] = zero * TILE
            cols[count] = 0
            sums[count] = which
            count = count + jnp.where(lax.rem(count, WIDE) > 0, 1, 0)
    bunches = lax.div(count, WIDE)

    def fetch(i, b, side):
        start = pl.multiple_of(cols[WIDE * i + side], TILE)
        return pltpu.make_async_copy(
            w.at[:, pl.ds(start, TILE)],
            held.at[b, :, pl.ds(side * TILE, TILE)],
            w_sem.at[b, side],
        )

    for b in range(DEPTH):

        @pl.when(b < bunches)
        def _():
            for side in range(WIDE):
                fetch(b, b, side).start()

    for arrive in arrives:
        arrive.wait()

    def one(i, carry):
        b = lax.rem(i, DEPTH)
        for side in range(WIDE):
            fetch(i, b, side).wait()
        picked = [
            tiles[pl.ds(pl.multiple_of(rows[WIDE * i + side], TILE), TILE), :]
            for side in range(WIDE)
        ]
        total[sums[WIDE * i]] += jnp.dot(
            held[b], jnp.concatenate(picked, axis=0), preferred_element_type=jnp.float32
        )

        @pl.when(i + DEPTH < bunches)
        def _():
            for side in range(WIDE):
                fetch(i + DEPTH, b, side).start()

        return carry

    lax.fori_loop(0, bunches, one, 0)
    own_a, own_b, up, down, next_b, last_a = outs
    x = lax.axis_index("x")

    def give(ref, at, away, side):
        first = lax.rem(x + away, X) * (2 * half) + side * half
        first = pl.multiple_of(first, half)
        for s in range(steps):
            for j in range(2):
                ref[at + s * half : at + (s + 1) * half, j * TILE : (j + 1) * TILE] = total[
                    s * 2 + j, pl.ds(first, half), :
                ]

    give(up, 0, 2, 1)
    give(up, steps * half, 1, 0)
    give(down, 0, 2, 0)
    give(down, steps * half, 3, 1)
    give(next_b, 0, 1, 1)
    give(last_a, 0, 3, 0)
    give(own_a, 0, 0, 0)
    give(own_b, 0, 0, 1)


def contract(begin, steps, got, w):
    vmem = pl.BlockSpec(memory_space=pltpu.VMEM)
    hbm = pl.BlockSpec(memory_space=pltpu.HBM)
    row_count = w.shape[0]
    half = row_count // X // 2
    slots = slots_of(steps)
    most = GROUP * slots + 2 * steps * WIDE
    one = jax.ShapeDtypeStruct((steps * half, 2 * TILE), jnp.float32)
    two = jax.ShapeDtypeStruct((2 * steps * half, 2 * TILE), jnp.float32)

    def kernel(*refs):
        contract_kernel(begin, steps, *refs)

    return pl.pallas_call(
        kernel,
        out_shape=[one, one, two, two, one, one],
        in_specs=[hbm, hbm],
        out_specs=[vmem] * 6,
        scratch_shapes=[
            pltpu.VMEM(((GROUP * slots + 1) * TILE, TILE), jnp.bfloat16),
            pltpu.VMEM((2 * steps, row_count, TILE), jnp.float32),
            pltpu.VMEM((DEPTH, row_count, WIDE * TILE), jnp.bfloat16),
            pltpu.VMEM((GROUP, META, TILE), jnp.bfloat16),
            pltpu.VMEM((GROUP, TILE), jnp.int32),
            pltpu.SMEM((GROUP, TILE), jnp.int32),
            pltpu.SMEM((most,), jnp.int32),
            pltpu.SMEM((most,), jnp.int32),
            pltpu.SMEM((most,), jnp.int32),
            pltpu.SemaphoreType.DMA((2 + GROUP,)),
            pltpu.SemaphoreType.DMA((DEPTH, WIDE)),
        ],
        compiler_params=pltpu.CompilerParams(vmem_limit_bytes=56 << 20),
        cost_estimate=pl.CostEstimate(flops=1 << 20, bytes_accessed=1 << 20, transcendentals=0),
        name="contract",
    )(got, w)


def local(t2_tiles, kc_tile, jb_tile, tile_owner, w_slices):
    half = w_slices.shape[0] // X // 2
    up_x = [(i, (i + 1) % X) for i in range(X)]
    down_x = [(i, (i - 1) % X) for i in range(X)]
    names = tile_owner.reshape(-1)
    gots = []
    for chunk in range(len(CHUNKS)):
        sent = route(chunk, kc_tile, jb_tile, names, t2_tiles)
        gots.append(lax.all_to_all(sent, ("zl", "y", "k"), split_axis=0, concat_axis=0, tiled=True))
    parts, before = [], []
    for chunk, begin, steps in CALLS:
        cut = steps * half
        got = lax.optimization_barrier((gots[chunk], *before))[0]
        own_a, own_b, up, down, next_b, last_a = contract(begin, steps, got, w_slices)
        from_low = lax.ppermute(up, "x", up_x)
        from_high = lax.ppermute(down, "x", down_x)
        next_b, last_a = next_b + from_low[:cut], last_a + from_high[:cut]
        before = [next_b, last_a]
        from_low_b = lax.ppermute(next_b, "x", up_x)
        from_high_a = lax.ppermute(last_a, "x", down_x)
        for s in range(steps):
            here = slice(s * half, (s + 1) * half)
            there = slice(cut + s * half, cut + (s + 1) * half)
            block_a = own_a[here] + from_low[there] + from_high_a[here]
            block_b = own_b[here] + from_high[there] + from_low_b[here]
            block = jnp.concatenate([block_a, block_b], axis=0)
            away = ORDER[FIRST[chunk] + begin + s]
            if away:
                block = lax.ppermute(block, "zh", [(i, (i + away) % HIGH) for i in range(HIGH)])
            parts.append(block)
    return sum(parts[1:], parts[0]).astype(jnp.bfloat16)


def solution(mesh):
    every = ("zh", "zl", "y", "k", "x")
    fine = Mesh(mesh.devices.reshape(HIGH, LOW, Y, K, X), every)
    return jax.shard_map(
        local,
        mesh=fine,
        in_specs=(
            P(every, None, None),
            P(every),
            P(every),
            P(every, None),
            P(None, "x"),
        ),
        out_specs=P("x", every[:4]),
        check_vma=False,
    )
```

time: 484 us -> 170 us (0.35); the launches traced: 479 us -> 170 us
  local copies, waits for them, and re-layouts: 128 us -> 0.01 us
  other arithmetic: 129 us -> 6.85 us
  matrix products: 70.3 us -> 0 us
  waiting for transfers between devices: 95.7 us -> 31.6 us
  blocking collectives: 33 us -> 78.4 us
  Pallas kernels: 0 us -> 26.4 us
    scatter-add x6 -> x0, other arithmetic: 126 us -> none  [one_block(): running = running.at[:, id_block[:, 1], :].add(product)]
    all_to_all x2 -> x0, waiting for transfers between devices: 95.7 us -> none  [the longest x1 95.7 us: local(): lax.all_to_all(send_tiles, 'pair', split_axis=0, concat_axis=0, tiled=True)]
    all_to_all x0 -> x1, blocking collectives: none -> 78.4 us  [local(): lax.all_to_all(sent, ('zl', 'y', 'k'), split_axis=0, concat_axis=0, tiled...]
    dot_general x6 -> x0, matrix products: 70.3 us -> none  [one_block(): jnp.einsum('rna,nab->rnb', picked, tile_block, preferred_element_type=jnp...]
    gather x6 -> x0, local copies, waits for them, and re-layouts: 64 us -> none  [one_block(): picked = jnp.take(w_blocks, id_block[:, 0], axis=1)]
    psum x1 -> x0, blocking collectives: 33 us -> none  [local(): summed = lax.psum(partial_sum, 'cuts')]
    ppermute x0 -> x11, waiting for transfers between devices: none -> 31.6 us  [the longest x2 19.8 us: local(): from_low = lax.ppermute(up, 'x', up_x)]
    ppermute x0 -> x11, starting transfers between devices: none -> 26.8 us  [the longest x3 13.5 us: local(): lax.ppermute(block, 'zh', [(i, (i + away) % HIGH) for i in range(HIGH)])]
  transfers between devices with their start and end apart: 2 -> 11, of which waited for: 1 -> 5; matrix products, arithmetic and copies ran while one was open for 13% -> 4% of each run, Pallas kernels for 0% -> 6%
where the time goes in v2:
time: 170 us
  blocking collectives  78.4 us (46%)
  waiting for transfers between devices  31.6 us (19%)
  starting transfers between devices  26.8 us (16%)
  Pallas kernels  26.4 us (16%)
  other arithmetic  6.85 us (4%)
    all_to_all x1, blocking collectives, local(): lax.all_to_all(sent, ('zl', 'y', 'k'), split_axis=0, concat_axis=0, tiled...  78.4 us
    pallas_call x2, Pallas kernels, contract(): pl.pallas_call(kernel, out_shape=[one, one, two, two, one, one], in_specs...  20.1 us
    ppermute x2, waiting for transfers between devices, local(): from_low = lax.ppermute(up, 'x', up_x)  19.8 us
    ppermute x3, starting transfers between devices, local(): lax.ppermute(block, 'zh', [(i, (i + away) % HIGH) for i in range(HIGH)])  13.5 us
    ppermute x3, waiting for transfers between devices, local(): lax.ppermute(block, 'zh', [(i, (i + away) % HIGH) for i in range(HIGH)])  10 us
    ppermute x2, starting transfers between devices, local(): from_high_a = lax.ppermute(last_a, 'x', down_x)  6.58 us
    pallas_call x1, Pallas kernels, route(): pl.pallas_call(kernel, out_shape=jax.ShapeDtypeStruct((GROUP, block_of(CH...  6.35 us
    ppermute x2, starting transfers between devices, local(): from_high = lax.ppermute(down, 'x', down_x)  5.7 us
  transfers between devices with their start and end apart: 11, of which 5 were waited for; matrix products, arithmetic and copies ran while one was open for 4% of the time, Pallas kernels for 6%

profile of v2, /device:TPU:32, one launch (start us, length us, event | category | flops | bytes accessed | tf_op | source)
XLA Modules:
  0.0 170.3 jit_solution(3143351253606039928)
XLA Ops:
  0.0 6.3 %route.1 = bf16[16,1552,128]{2,1,0:T(8,128)(2,1)} custom-call(s32[96]{0:T(128)} %refs_0_.1, s32[96]{0:T(128)} %refs_1_.3, s32[96]{0:T(128)} %bitcast.1, bf16[96,128,128]{2,1,0:T(8,128)(2,1)} %refs_3_.1), custom_call_target="tpu_custom_call" | custom-call | bytes 8388608 | tf_op jit(solution)/shard_map/route/pallas_call | solution.py:92
  6.4 78.4 %all_to_all.5.refs_0_ = bf16[16,1552,128]{2,1,0:T(8,128)(2,1)} all-to-all(bf16[16,1552,128]{2,1,0:T(8,128)(2,1)} %route.1), channel_id=1, replica_groups=mesh['zh'=4,'zl'=2,'y'=4,'k'=2,'x'=4] {'zl','y','k'}, dimensions={0} | all-to-all | bytes 12713984 | tf_op jit(solution)/shard_map/all_to_all | solution.py:261
  84.8 10.0 %contract.2 = (f32[256,256]{1,0:T(8,128)}, f32[256,256]{1,0:T(8,128)}, f32[512,256]{1,0:T(8,128)}, f32[512,256]{1,0:T(8,128)}, f32[256,256]{1,0:T(8,128)}, /*index=5*/f32[256,256]{1,0:T(8,128)}) custom-call(bf16[16,1552,128]{2,1,0:T(8,128)(2,1)} %all_to_all.5.refs_0_, bf16[1024,8192]{1,0:T(8,128)(2,1)} %refs_1_.5), custom_call_target="tpu_custom_call" | custom-call | flops 1048576 | bytes 1048576 | tf_op jit(solution)/shard_map/contract/pallas_call | solution.py:229
  94.8 0.8 collective-permute-start
  95.7 2.5 %collective-permute-start.1 = (f32[512,256]{1,0:T(8,128)}, f32[512,256]{1,0:T(8,128)S(1)}, u32[]{:S(2)}, u32[]{:S(2)}) collective-permute-start(f32[512,256]{1,0:T(8,128)} %get-tuple-element.21), channel_id=1, source_target_pairs={{0,3},{1,0},{2,1},{3,2},{4,7},{5,4},{6,5},{7,6},{8,11},{9,8},{10,9... | collective-permute-start | bytes 1572872 | tf_op jit(solution)/shard_map/ppermute | solution.py:268
  98.1 12.1 %collective-permute-done = f32[512,256]{1,0:T(8,128)S(1)} collective-permute-done((f32[512,256]{1,0:T(8,128)}, f32[512,256]{1,0:T(8,128)S(1)}, u32[]{:S(2)}, u32[]{:S(2)}) %collective-permute-start) | collective-permute-done | bytes 524320 | tf_op jit(solution)/shard_map/ppermute | solution.py:267
  110.2 1.0 slice_add_fusion.2
  111.3 1.0 slice_add_fusion.3
  112.3 3.3 %collective-permute-start.2 = (f32[256,256]{1,0:T(8,128)S(1)}, f32[256,256]{1,0:T(8,128)S(1)}, u32[]{:S(2)}, u32[]{:S(2)}) collective-permute-start(f32[256,256]{1,0:T(8,128)S(1)} %slice_add_fusion.3), channel_id=1, source_target_pairs={{0,3},{1,0},{2,1},{3,2},{4,7},{5,4},{6,5},{7,6},{8,11},{9,8},{10,9... | collective-permute-start | bytes 786440 | tf_op jit(solution)/shard_map/ppermute | solution.py:272
  115.6 10.0 %contract.3 = (f32[256,256]{1,0:T(8,128)}, f32[256,256]{1,0:T(8,128)}, f32[512,256]{1,0:T(8,128)}, f32[512,256]{1,0:T(8,128)}, f32[256,256]{1,0:T(8,128)}, /*index=5*/f32[256,256]{1,0:T(8,128)}) custom-call(bf16[16,1552,128]{2,1,0:T(8,128)(2,1)} %all_to_all.5.refs_0_, bf16[1024,8192]{1,0:T(8,128)(2,1)} %refs_1_.5), custom_call_target="tpu_custom_call" | custom-call | flops 1048576 | bytes 1048576 | tf_op jit(solution)/shard_map/contract/pallas_call | solution.py:229
  125.8 3.2 %collective-permute-start.7 = (f32[512,256]{1,0:T(8,128)}, f32[512,256]{1,0:T(8,128)S(1)}, u32[]{:S(2)}, u32[]{:S(2)}) collective-permute-start(f32[512,256]{1,0:T(8,128)} %get-tuple-element.28), channel_id=1, source_target_pairs={{0,3},{1,0},{2,1},{3,2},{4,7},{5,4},{6,5},{7,6},{8,11},{9,8},{10,9... | collective-permute-start | bytes 1572872 | tf_op jit(solution)/shard_map/ppermute | solution.py:268
  129.2 3.7 %collective-permute-start.4 = (f32[256,256]{1,0:T(8,128)S(1)}, f32[256,256]{1,0:T(8,128)S(1)}, u32[]{:S(2)}, u32[]{:S(2)}) collective-permute-start(f32[256,256]{1,0:T(8,128)S(1)} %pad_maximum_fusion), channel_id=1, source_target_pairs={{0,128},{64,192},{128,0},{192,64},{1,129},{65,193},{129,1},{193,65... | collective-permute-start | bytes 786440 | tf_op jit(solution)/shard_map/ppermute | solution.py:281
  132.9 7.7 %collective-permute-done.6 = f32[512,256]{1,0:T(8,128)S(1)} collective-permute-done((f32[512,256]{1,0:T(8,128)}, f32[512,256]{1,0:T(8,128)S(1)}, u32[]{:S(2)}, u32[]{:S(2)}) %collective-permute-start.6) | collective-permute-done | bytes 524320 | tf_op jit(solution)/shard_map/ppermute | solution.py:267
  140.6 1.0 slice_add_fusion
  141.7 1.0 slice_add_fusion.1
  142.7 3.3 %collective-permute-start.8 = (f32[256,256]{1,0:T(8,128)S(1)}, f32[256,256]{1,0:T(8,128)S(1)}, u32[]{:S(2)}, u32[]{:S(2)}) collective-permute-start(f32[256,256]{1,0:T(8,128)S(1)} %slice_add_fusion.1), channel_id=1, source_target_pairs={{0,3},{1,0},{2,1},{3,2},{4,7},{5,4},{6,5},{7,6},{8,11},{9,8},{10,9... | collective-permute-start | bytes 786440 | tf_op jit(solution)/shard_map/ppermute | solution.py:272
  146.0 4.0 %collective-permute-start.5 = (f32[256,256]{1,0:T(8,128)S(1)}, f32[256,256]{1,0:T(8,128)S(1)}, u32[]{:S(2)}, u32[]{:S(2)}) collective-permute-start(f32[256,256]{1,0:T(8,128)S(1)} %pad_maximum_fusion.1), channel_id=1, source_target_pairs={{0,64},{64,128},{128,192},{192,0},{1,65},{65,129},{129,193},{193,1... | collective-permute-start | bytes 786440 | tf_op jit(solution)/shard_map/ppermute | solution.py:281
  150.0 1.7 collective-permute-done.9
  151.7 1.0 slice_add_fusion.8
  152.7 1.0 slice_add_fusion.10
  153.8 5.7 %collective-permute-start.10 = (f32[256,256]{1,0:T(8,128)S(1)}, f32[256,256]{1,0:T(8,128)S(1)}, u32[]{:S(2)}, u32[]{:S(2)}) collective-permute-start(f32[256,256]{1,0:T(8,128)S(1)} %pad_maximum_fusion.2), channel_id=1, source_target_pairs={{0,192},{64,0},{128,64},{192,128},{1,193},{65,1},{129,65},{193,129... | collective-permute-start | bytes 786440 | tf_op jit(solution)/shard_map/ppermute | solution.py:281
  159.5 2.4 %collective-permute-done.5 = f32[256,256]{1,0:T(8,128)S(1)} collective-permute-done((f32[256,256]{1,0:T(8,128)S(1)}, f32[256,256]{1,0:T(8,128)S(1)}, u32[]{:S(2)}, u32[]{:S(2)}) %collective-permute-start.5) | collective-permute-done | bytes 262176 | tf_op jit(solution)/shard_map/ppermute | solution.py:281
  161.9 7.7 %collective-permute-done.10 = f32[256,256]{1,0:T(8,128)S(1)} collective-permute-done((f32[256,256]{1,0:T(8,128)S(1)}, f32[256,256]{1,0:T(8,128)S(1)}, u32[]{:S(2)}, u32[]{:S(2)}) %collective-permute-start.10) | collective-permute-done | bytes 262176 | tf_op jit(solution)/shard_map/ppermute | solution.py:281
  169.6 0.7 fusion
  (18 shorter events, 0.4 us)
Async XLA Ops:
  94.8 15.4 %collective-permute-start = (f32[512,256]{1,0:T(8,128)}, f32[512,256]{1,0:T(8,128)S(1)}, u32[]{:S(2)}, u32[]{:S(2)}) collective-permute-start(f32[512,256]{1,0:T(8,128)} %get-tuple-element.19), channel_id=1, source_target_pairs={{0,1},{1,2},{2,3},{3,0},{4,5},{5,6},{6,7},{7,4},{8,9},{9,10},{10,1... | collective-permute-start | bytes 1572872 | tf_op jit(solution)/shard_map/ppermute | solution.py:267
  95.7 15.7 %collective-permute-start.1 = (f32[512,256]{1,0:T(8,128)}, f32[512,256]{1,0:T(8,128)S(1)}, u32[]{:S(2)}, u32[]{:S(2)}) collective-permute-start(f32[512,256]{1,0:T(8,128)} %get-tuple-element.21), channel_id=1, source_target_pairs={{0,3},{1,0},{2,1},{3,2},{4,7},{5,4},{6,5},{7,6},{8,11},{9,8},{10,9... | collective-permute-start | bytes 1572872 | tf_op jit(solution)/shard_map/ppermute | solution.py:268
  111.2 17.8 %collective-permute-start.3 = (f32[256,256]{1,0:T(8,128)S(1)}, f32[256,256]{1,0:T(8,128)S(1)}, u32[]{:S(2)}, u32[]{:S(2)}) collective-permute-start(f32[256,256]{1,0:T(8,128)S(1)} %slice_add_fusion.2), channel_id=1, source_target_pairs={{0,1},{1,2},{2,3},{3,0},{4,5},{5,6},{6,7},{7,4},{8,9},{9,10},{10,1... | collective-permute-start | bytes 786440 | tf_op jit(solution)/shard_map/ppermute | solution.py:271
  112.3 16.7 %copy-start.1 = (f32[256,256]{1,0:T(8,128)S(1)}, f32[256,256]{1,0:T(8,128)}, u32[]{:S(2)}) copy-start(f32[256,256]{1,0:T(8,128)} %get-tuple-element.22) | copy-start | bytes 786436
  112.3 16.7 %copy-start = (f32[256,256]{1,0:T(8,128)S(1)}, f32[256,256]{1,0:T(8,128)}, u32[]{:S(2)}) copy-start(f32[256,256]{1,0:T(8,128)} %get-tuple-element.18) | copy-start | bytes 786436
  112.3 16.7 %collective-permute-start.2 = (f32[256,256]{1,0:T(8,128)S(1)}, f32[256,256]{1,0:T(8,128)S(1)}, u32[]{:S(2)}, u32[]{:S(2)}) collective-permute-start(f32[256,256]{1,0:T(8,128)S(1)} %slice_add_fusion.3), channel_id=1, source_target_pairs={{0,3},{1,0},{2,1},{3,2},{4,7},{5,4},{6,5},{7,6},{8,11},{9,8},{10,9... | collective-permute-start | bytes 786440 | tf_op jit(solution)/shard_map/ppermute | solution.py:272
  125.7 15.0 %collective-permute-start.6 = (f32[512,256]{1,0:T(8,128)}, f32[512,256]{1,0:T(8,128)S(1)}, u32[]{:S(2)}, u32[]{:S(2)}) collective-permute-start(f32[512,256]{1,0:T(8,128)} %get-tuple-element.26), channel_id=1, source_target_pairs={{0,1},{1,2},{2,3},{3,0},{4,5},{5,6},{6,7},{7,4},{8,9},{9,10},{10,1... | collective-permute-start | bytes 1572872 | tf_op jit(solution)/shard_map/ppermute | solution.py:267
  125.8 16.0 %collective-permute-start.7 = (f32[512,256]{1,0:T(8,128)}, f32[512,256]{1,0:T(8,128)S(1)}, u32[]{:S(2)}, u32[]{:S(2)}) collective-permute-start(f32[512,256]{1,0:T(8,128)} %get-tuple-element.28), channel_id=1, source_target_pairs={{0,3},{1,0},{2,1},{3,2},{4,7},{5,4},{6,5},{7,6},{8,11},{9,8},{10,9... | collective-permute-start | bytes 1572872 | tf_op jit(solution)/shard_map/ppermute | solution.py:268
  129.2 30.3 %collective-permute-start.4 = (f32[256,256]{1,0:T(8,128)S(1)}, f32[256,256]{1,0:T(8,128)S(1)}, u32[]{:S(2)}, u32[]{:S(2)}) collective-permute-start(f32[256,256]{1,0:T(8,128)S(1)} %pad_maximum_fusion), channel_id=1, source_target_pairs={{0,128},{64,192},{128,0},{192,64},{1,129},{65,193},{129,1},{193,65... | collective-permute-start | bytes 786440 | tf_op jit(solution)/shard_map/ppermute | solution.py:281
  141.6 10.1 %collective-permute-start.9 = (f32[256,256]{1,0:T(8,128)S(1)}, f32[256,256]{1,0:T(8,128)S(1)}, u32[]{:S(2)}, u32[]{:S(2)}) collective-permute-start(f32[256,256]{1,0:T(8,128)S(1)} %slice_add_fusion), channel_id=1, source_target_pairs={{0,1},{1,2},{2,3},{3,0},{4,5},{5,6},{6,7},{7,4},{8,9},{9,10},{10,1... | collective-permute-start | bytes 786440 | tf_op jit(solution)/shard_map/ppermute | solution.py:271
  142.7 10.0 %collective-permute-start.8 = (f32[256,256]{1,0:T(8,128)S(1)}, f32[256,256]{1,0:T(8,128)S(1)}, u32[]{:S(2)}, u32[]{:S(2)}) collective-permute-start(f32[256,256]{1,0:T(8,128)S(1)} %slice_add_fusion.1), channel_id=1, source_target_pairs={{0,3},{1,0},{2,1},{3,2},{4,7},{5,4},{6,5},{7,6},{8,11},{9,8},{10,9... | collective-permute-start | bytes 786440 | tf_op jit(solution)/shard_map/ppermute | solution.py:272
  146.0 15.9 %collective-permute-start.5 = (f32[256,256]{1,0:T(8,128)S(1)}, f32[256,256]{1,0:T(8,128)S(1)}, u32[]{:S(2)}, u32[]{:S(2)}) collective-permute-start(f32[256,256]{1,0:T(8,128)S(1)} %pad_maximum_fusion.1), channel_id=1, source_target_pairs={{0,64},{64,128},{128,192},{192,0},{1,65},{65,129},{129,193},{193,1... | collective-permute-start | bytes 786440 | tf_op jit(solution)/shard_map/ppermute | solution.py:281
  153.8 15.8 %collective-permute-start.10 = (f32[256,256]{1,0:T(8,128)S(1)}, f32[256,256]{1,0:T(8,128)S(1)}, u32[]{:S(2)}, u32[]{:S(2)}) collective-permute-start(f32[256,256]{1,0:T(8,128)S(1)} %pad_maximum_fusion.2), channel_id=1, source_target_pairs={{0,192},{64,0},{128,64},{192,128},{1,193},{65,1},{129,65},{193,129... | collective-permute-start | bytes 786440 | tf_op jit(solution)/shard_map/ppermute | solution.py:281

commit v3 on v2

--- a/solution.py
+++ b/solution.py
@@ -14,9 +14,8 @@
 DEPTH = 4
 WIDE = 4
 ORDER = (2, 1, 3, 0)
-CHUNKS = (4,)
-FIRST = (0,)
-CALLS = ((0, 0, 2), (0, 2, 2))
+CHUNKS = (3, 1)
+FIRST = (0, 3)
 
 
 def slots_of(steps):
@@ -27,10 +26,10 @@
     return slots_of(steps) * TILE + META
 
 
-def route_kernel(chunk, kc, jb, owner, tiles, send, *scratch):
+def route_kernel(kc, jb, owner, tiles, *rest):
+    sends, scratch = rest[: len(CHUNKS)], rest[len(CHUNKS) :]
     kc_s, jb_s, owner_s, counts, codes, kind_sem, sem = scratch
     held = tiles.shape[0]
-    steps = CHUNKS[chunk]
     loads = [
         pltpu.make_async_copy(a, b, kind_sem.at[i])
         for i, (a, b) in enumerate(((kc, kc_s), (jb, jb_s), (owner, owner_s)))
@@ -49,51 +48,46 @@
     for load in loads:
         load.wait()
 
-    def one(i, sent):
+    def one(i, carry):
         name = owner_s[i]
         away = (lax.shift_right_logical(name, 4) - high) & (HIGH - 1)
-        step = jnp.int32(-1)
-        for s in range(steps):
-            step = jnp.where(away == ORDER[FIRST[chunk] + s], s, step)
-
-        @pl.when(step >= 0)
-        def _():
-            rank = counts[name]
-            counts[name] = rank + 1
-            dest = name & (GROUP - 1)
-            slot = step * CAP + rank
-            row = pl.multiple_of(slot * TILE, TILE)
-            pltpu.make_async_copy(tiles.at[i], send.at[dest, pl.ds(row, TILE), :], sem).start()
-            line = pl.ds(dest, 1)
-            code = (kc_s[i] * 2 + jb_s[i]).astype(jnp.float32)
-            codes[line, :] = jnp.where(lane == slot, code, codes[line, :])
-
-        return sent + jnp.where(step >= 0, 1, 0)
-
-    sent = lax.fori_loop(0, held, one, 0)
-    send[:, slots_of(steps) * TILE :, :] = jnp.broadcast_to(
-        codes[...][:, None, :], (GROUP, META, TILE)
-    ).astype(send.dtype)
-
-    def arrived(i, carry):
-        pltpu.make_async_copy(tiles.at[0], send.at[0, pl.ds(0, TILE), :], sem).wait()
+        step = jnp.int32(0)
+        for s in range(1, HIGH):
+            step = jnp.where(away == ORDER[s], s, step)
+        rank = counts[name]
+        counts[name] = rank + 1
+        dest = name & (GROUP - 1)
+        for c, send in enumerate(sends):
+
+            @pl.when((step >= FIRST[c]) & (step < FIRST[c] + CHUNKS[c]))
+            def _():
+                row = pl.multiple_of(((step - FIRST[c]) * CAP + rank) * TILE, TILE)
+                pltpu.make_async_copy(tiles.at[i], send.at[dest, pl.ds(row, TILE), :], sem).start()
+
+        line = pl.ds(dest, 1)
+        code = (kc_s[i] * 2 + jb_s[i]).astype(jnp.float32)
+        codes[line, :] = jnp.where(lane == step * CAP + rank, code, codes[line, :])
         return carry
 
-    lax.fori_loop(0, sent, arrived, 0)
-
-
-def route(chunk, kc, jb, owner, tiles):
+    lax.fori_loop(0, held, one, 0)
+    for c, send in enumerate(sends):
+        found = codes[...]
+        if FIRST[c]:
+            found = pltpu.roll(found, TILE - FIRST[c] * CAP, axis=1)
+        send[:, slots_of(CHUNKS[c]) * TILE :, :] = jnp.broadcast_to(
+            found[:, None, :], (GROUP, META, TILE)
+        ).astype(send.dtype)
+    pltpu.make_async_copy(tiles, tiles, sem).wait()
+
+
+def route(kc, jb, owner, tiles):
     hbm = pl.BlockSpec(memory_space=pltpu.HBM)
     held = tiles.shape[0]
-
-    def kernel(*refs):
-        route_kernel(chunk, *refs)
-
     return pl.pallas_call(
-        kernel,
-        out_shape=jax.ShapeDtypeStruct((GROUP, block_of(CHUNKS[chunk]), TILE), tiles.dtype),
+        route_kernel,
+        out_shape=[jax.ShapeDtypeStruct((GROUP, block_of(n), TILE), tiles.dtype) for n in CHUNKS],
         in_specs=[hbm] * 4,
-        out_specs=pl.BlockSpec(memory_space=pltpu.VMEM),
+        out_specs=[pl.BlockSpec(memory_space=pltpu.VMEM)] * len(CHUNKS),
         scratch_shapes=[
             pltpu.SMEM((held,), jnp.int32),
             pltpu.SMEM((held,), jnp.int32),
@@ -109,9 +103,10 @@
     )(kc, jb, owner, tiles)
 
 
-def contract_kernel(begin, steps, got, w, *rest):
-    outs = rest[:6]
-    tiles, total, held, codes_b, codes_v, codes, rows, cols, sums, sems, w_sem = rest[6:]
+def contract_kernel(steps, direct, got, w, *rest):
+    many = 4 if direct else 6
+    outs = rest[:many]
+    tiles, total, held, codes_b, codes_v, codes, rows, cols, sums, sems, w_sem = rest[many:]
     row_count = w.shape[0]
     half = row_count // X // 2
     slots = slots_of(steps)
@@ -122,7 +117,7 @@
     for j in range(GROUP):
         arrives.append(
             pltpu.make_async_copy(
-                got.at[j, pl.ds(begin * CAP * TILE, slots * TILE), :],
+                got.at[j, pl.ds(0, slots * TILE), :],
                 tiles.at[pl.ds(j * slots * TILE, slots * TILE), :],
                 sems.at[2 + j],
             )
@@ -141,7 +136,7 @@
         for j in range(GROUP):
             for rank in range(CAP):
                 slot = which // 2 * CAP + rank
-                code = codes[j, begin * CAP + slot]
+                code = codes[j, slot]
                 rows[count] = (j * slots + slot) * TILE
                 cols[count] = lax.shift_right_arithmetic(code, 1) * TILE
                 sums[count] = which
@@ -191,7 +186,6 @@
         return carry
 
     lax.fori_loop(0, bunches, one, 0)
-    own_a, own_b, up, down, next_b, last_a = outs
     x = lax.axis_index("x")
 
     def give(ref, at, away, side):
@@ -203,6 +197,12 @@
                     s * 2 + j, pl.ds(first, half), :
                 ]
 
+    if direct:
+        for away in range(X):
+            give(outs[away], 0, away, 0)
+            give(outs[away], steps * half, away, 1)
+        return
+    own_a, own_b, up, down, next_b, last_a = outs
     give(up, 0, 2, 1)
     give(up, steps * half, 1, 0)
     give(down, 0, 2, 0)
@@ -213,7 +213,7 @@
     give(own_b, 0, 0, 1)
 
 
-def contract(begin, steps, got, w):
+def contract(steps, direct, got, w):
     vmem = pl.BlockSpec(memory_space=pltpu.VMEM)
     hbm = pl.BlockSpec(memory_space=pltpu.HBM)
     row_count = w.shape[0]
@@ -223,14 +223,16 @@
     one = jax.ShapeDtypeStruct((steps * half, 2 * TILE), jnp.float32)
     two = jax.ShapeDtypeStruct((2 * steps * half, 2 * TILE), jnp.float32)
 
+    outs = [two] * X if direct else [one, one, two, two, one, one]
+
     def kernel(*refs):
-        contract_kernel(begin, steps, *refs)
+        contract_kernel(steps, direct, *refs)
 
     return pl.pallas_call(
         kernel,
-        out_shape=[one, one, two, two, one, one],
+        out_shape=outs,
         in_specs=[hbm, hbm],
-        out_specs=[vmem] * 6,
+        out_specs=[vmem] * len(outs),
         scratch_shapes=[
             pltpu.VMEM(((GROUP * slots + 1) * TILE, TILE), jnp.bfloat16),
             pltpu.VMEM((2 * steps, row_count, TILE), jnp.float32),
@@ -255,31 +257,46 @@
     up_x = [(i, (i + 1) % X) for i in range(X)]
     down_x = [(i, (i - 1) % X) for i in range(X)]
     names = tile_owner.reshape(-1)
-    gots = []
-    for chunk in range(len(CHUNKS)):
-        sent = route(chunk, kc_tile, jb_tile, names, t2_tiles)
-        gots.append(lax.all_to_all(sent, ("zl", "y", "k"), split_axis=0, concat_axis=0, tiled=True))
-    parts, before = [], []
-    for chunk, begin, steps in CALLS:
+    gots = [
+        lax.all_to_all(sent, ("zl", "y", "k"), split_axis=0, concat_axis=0, tiled=True)
+        for sent in route(kc_tile, jb_tile, names, t2_tiles)
+    ]
+
+    def join(steps, sums):
+        own_a, own_b, up, down, next_b, last_a = sums
         cut = steps * half
-        got = lax.optimization_barrier((gots[chunk], *before))[0]
-        own_a, own_b, up, down, next_b, last_a = contract(begin, steps, got, w_slices)
         from_low = lax.ppermute(up, "x", up_x)
         from_high = lax.ppermute(down, "x", down_x)
         next_b, last_a = next_b + from_low[:cut], last_a + from_high[:cut]
-        before = [next_b, last_a]
+        return next_b, last_a, own_a, own_b, from_low, from_high
+
+    def blocks(steps, joined):
+        next_b, last_a, own_a, own_b, from_low, from_high = joined
         from_low_b = lax.ppermute(next_b, "x", up_x)
         from_high_a = lax.ppermute(last_a, "x", down_x)
+        done = []
         for s in range(steps):
             here = slice(s * half, (s + 1) * half)
-            there = slice(cut + s * half, cut + (s + 1) * half)
+            there = slice((steps + s) * half, (steps + s + 1) * half)
             block_a = own_a[here] + from_low[there] + from_high_a[here]
             block_b = own_b[here] + from_high[there] + from_low_b[here]
-            block = jnp.concatenate([block_a, block_b], axis=0)
-            away = ORDER[FIRST[chunk] + begin + s]
-            if away:
-                block = lax.ppermute(block, "zh", [(i, (i + away) % HIGH) for i in range(HIGH)])
-            parts.append(block)
+            done.append(jnp.concatenate([block_a, block_b], axis=0))
+        return done
+
+    def send(block, away):
+        if not away:
+            return block
+        return lax.ppermute(block, "zh", [(i, (i + away) % HIGH) for i in range(HIGH)])
+
+    steps = CHUNKS[0]
+    first = contract(steps, False, gots[0], w_slices)
+    own, after, far, behind = contract(CHUNKS[1], True, gots[1], w_slices)
+    first = join(steps, first)
+    low_b, high_a, after, behind, far = lax.optimization_barrier((*first[:2], after, behind, far))
+    early = blocks(steps, (low_b, high_a, *first[2:]))
+    parts = [send(b, ORDER[s]) for s, b in enumerate(early)]
+    parts += [own, lax.ppermute(after, "x", up_x), lax.ppermute(behind, "x", down_x)]
+    parts += [lax.ppermute(far, "x", [(i, (i + 2) % X) for i in range(X)])]
     return sum(parts[1:], parts[0]).astype(jnp.bfloat16)
 
 

time: 170 us -> 155 us (0.912); the launches traced: 170 us -> 152 us
  blocking collectives: 78.4 us -> 61.5 us
  Pallas kernels: 26.4 us -> 32.8 us
  other arithmetic: 6.85 us -> 1.06 us
  waiting for transfers between devices: 31.6 us -> 27 us
  starting transfers between devices: 26.8 us -> 28.6 us
    all_to_all x1, blocking collectives: 78.4 us -> 61.5 us  [local(): lax.all_to_all(sent, ('zl', 'y', 'k'), split_axis=0, concat_axis=0, tiled...]
    pallas_call x3, Pallas kernels: 26.4 us -> 32.8 us  [the longest x2 26.8 us: contract(): pl.pallas_call(kernel, out_shape=outs, in_specs=[hbm, hbm], out_specs=[vm...]
    add x8 -> x4, other arithmetic: 6.09 us -> 0.25 us  [the longest x2 0.1 us: join(): next_b, last_a = (next_b + from_low[:cut], last_a + from_high[:cut])]
    all_to_all x0 -> x1, starting transfers between devices: none -> 4.99 us  [local(): lax.all_to_all(sent, ('zl', 'y', 'k'), split_axis=0, concat_axis=0, tiled...]
    ppermute x11 -> x10, waiting for transfers between devices: 31.6 us -> 26.7 us  [the longest x3 11.5 us: send(): lax.ppermute(block, 'zh', [(i, (i + away) % HIGH) for i in range(HIGH)])]
    ppermute x11 -> x10, starting transfers between devices: 26.8 us -> 23.7 us  [the longest x3 12.6 us: send(): lax.ppermute(block, 'zh', [(i, (i + away) % HIGH) for i in range(HIGH)])]
  transfers between devices with their start and end apart: 11 -> 11, of which waited for: 5 -> 7; matrix products, arithmetic and copies ran while one was open for 4% -> 0% of each run, Pallas kernels for 6% -> 18%
where the time goes in v3:
time: 155 us; the launch traced here: 152 us
  blocking collectives  61.5 us (40%)
  Pallas kernels  32.8 us (21%)
  starting transfers between devices  28.6 us (18%)
  waiting for transfers between devices  27 us (17%)
    all_to_all x1, blocking collectives, local(): lax.all_to_all(sent, ('zl', 'y', 'k'), split_axis=0, concat_axis=0, tiled...  61.5 us
    pallas_call x2, Pallas kernels, contract(): pl.pallas_call(kernel, out_shape=outs, in_specs=[hbm, hbm], out_specs=[vm...  26.8 us
    ppermute x3, starting transfers between devices, send(): lax.ppermute(block, 'zh', [(i, (i + away) % HIGH) for i in range(HIGH)])  12.6 us
    ppermute x3, waiting for transfers between devices, send(): lax.ppermute(block, 'zh', [(i, (i + away) % HIGH) for i in range(HIGH)])  11.5 us
    ppermute x1, waiting for transfers between devices, join(): from_low = lax.ppermute(up, 'x', up_x)  6.13 us
    pallas_call x1, Pallas kernels, route(): pl.pallas_call(route_kernel, out_shape=[jax.ShapeDtypeStruct((GROUP, bloc...  5.99 us
    ppermute x1, waiting for transfers between devices, blocks(): from_high_a = lax.ppermute(last_a, 'x', down_x)  5.83 us
    all_to_all x1, starting transfers between devices, local(): lax.all_to_all(sent, ('zl', 'y', 'k'), split_axis=0, concat_axis=0, tiled...  4.99 us
  transfers between devices with their start and end apart: 11, of which 7 were waited for; matrix products, arithmetic and copies ran while one was open for 0% of the time, Pallas kernels for 18%

profile of v3, /device:TPU:32, one launch (start us, length us, event | category | flops | bytes accessed | tf_op | source)
XLA Modules:
  0.0 152.3 jit_solution(14051809824564669187)
XLA Ops:
  0.0 6.0 %route.1 = (bf16[16,1168,128]{2,1,0:T(8,128)(2,1)}, bf16[16,400,128]{2,1,0:T(8,128)(2,1)}) custom-call(s32[96]{0:T(128)} %kc.1, s32[96]{0:T(128)} %jb.1, s32[96]{0:T(128)} %bitcast.1, bf16[96,128,128]{2,1,0:T(8,128)(2,1)} %tiles.1), custom_call_target="tpu_custom_call" | custom-call | bytes 8388608 | tf_op jit(solution)/shard_map/route/pallas_call | solution.py:86
  6.0 61.5 %all_to_all.10.refs_0_ = bf16[16,1168,128]{2,1,0:T(8,128)(2,1)} all-to-all(bf16[16,1168,128]{2,1,0:T(8,128)(2,1)} %get-tuple-element.22), channel_id=1, replica_groups=mesh['zh'=4,'zl'=2,'y'=4,'k'=2,'x'=4] {'zl','y','k'}, dimensions={0} | all-to-all | bytes 9568256 | tf_op jit(solution)/shard_map/all_to_all | solution.py:261
  67.5 5.0 %all-to-all-start.1 = ((bf16[16,400,128]{2,1,0:T(8,128)(2,1)}), bf16[16,400,128]{2,1,0:T(8,128)(2,1)S(1)}, u32[]{:S(2)}, u32[]{:S(2)}) async-start(bf16[16,400,128]{2,1,0:T(8,128)(2,1)} %get-tuple-element.28), calls=%async_computation.1 | async-start | bytes 3276800 | tf_op jit(solution)/shard_map/all_to_all | solution.py:261
  72.5 18.1 %contract.2 = (f32[384,256]{1,0:T(8,128)}, f32[384,256]{1,0:T(8,128)}, f32[768,256]{1,0:T(8,128)}, f32[768,256]{1,0:T(8,128)}, f32[384,256]{1,0:T(8,128)}, /*index=5*/f32[384,256]{1,0:T(8,128)}) custom-call(bf16[16,1168,128]{2,1,0:T(8,128)(2,1)} %all_to_all.10.refs_0_, bf16[1024,8192]{1,0:T(8,128)(2,1)} %refs_1_.3), custom_call_target="tpu_custom_call" | custom-call | flops 1048576 | bytes 1048576 | tf_op jit(solution)/shard_map/contract/pallas_call | solution.py:231
  90.6 1.7 %collective-permute-start = (f32[768,256]{1,0:T(8,128)}, f32[768,256]{1,0:T(8,128)S(1)}, u32[]{:S(2)}, u32[]{:S(2)}) collective-permute-start(f32[768,256]{1,0:T(8,128)} %get-tuple-element.24), channel_id=1, source_target_pairs={{0,1},{1,2},{2,3},{3,0},{4,5},{5,6},{6,7},{7,4},{8,9},{9,10},{10,1... | collective-permute-start | bytes 2359304 | tf_op jit(solution)/shard_map/ppermute | solution.py:268
  92.3 1.6 %collective-permute-start.1 = (f32[768,256]{1,0:T(8,128)}, f32[768,256]{1,0:T(8,128)S(1)}, u32[]{:S(2)}, u32[]{:S(2)}) collective-permute-start(f32[768,256]{1,0:T(8,128)} %get-tuple-element.27), channel_id=1, source_target_pairs={{0,3},{1,0},{2,1},{3,2},{4,7},{5,4},{6,5},{7,6},{8,11},{9,8},{10,9... | collective-permute-start | bytes 2359304 | tf_op jit(solution)/shard_map/ppermute | solution.py:269
  93.9 0.4 all-to-all-done.1.refs_0_
  94.2 1.2 copy-done
  95.5 8.7 %contract.3 = (f32[256,256]{1,0:T(8,128)}, f32[256,256]{1,0:T(8,128)}, f32[256,256]{1,0:T(8,128)}, f32[256,256]{1,0:T(8,128)}) custom-call(bf16[16,400,128]{2,1,0:T(8,128)(2,1)} %copy-done, bf16[1024,8192]{1,0:T(8,128)(2,1)} %refs_1_.3), custom_call_target="tpu_custom_call" | custom-call | flops 1048576 | bytes 1048576 | tf_op jit(solution)/shard_map/contract/pallas_call | solution.py:231
  104.2 6.1 %collective-permute-done = f32[768,256]{1,0:T(8,128)S(1)} collective-permute-done((f32[768,256]{1,0:T(8,128)}, f32[768,256]{1,0:T(8,128)S(1)}, u32[]{:S(2)}, u32[]{:S(2)}) %collective-permute-start) | collective-permute-done | bytes 786464 | tf_op jit(solution)/shard_map/ppermute | solution.py:268
  110.4 3.1 %collective-permute-start.2 = (f32[384,256]{1,0:T(8,128)S(1)}, f32[384,256]{1,0:T(8,128)S(1)}, u32[]{:S(2)}, u32[]{:S(2)}) collective-permute-start(f32[384,256]{1,0:T(8,128)S(1)} %slice_add_fusion), channel_id=1, source_target_pairs={{0,3},{1,0},{2,1},{3,2},{4,7},{5,4},{6,5},{7,6},{8,11},{9,8},{10,9... | collective-permute-start | bytes 1179656 | tf_op jit(solution)/shard_map/ppermute | solution.py:276
  113.5 0.1 collective-permute-start.7
  113.6 3.2 %collective-permute-start.8 = (f32[256,256]{1,0:T(8,128)}, f32[256,256]{1,0:T(8,128)S(1)}, u32[]{:S(2)}, u32[]{:S(2)}) collective-permute-start(f32[256,256]{1,0:T(8,128)} %get-tuple-element.37), channel_id=1, source_target_pairs={{0,3},{1,0},{2,1},{3,2},{4,7},{5,4},{6,5},{7,6},{8,11},{9,8},{10,9... | collective-permute-start | bytes 786440 | tf_op jit(solution)/shard_map/ppermute | solution.py:298
  116.8 1.4 collective-permute-start.9
  118.2 5.8 %collective-permute-done.2 = f32[384,256]{1,0:T(8,128)S(1)} collective-permute-done((f32[384,256]{1,0:T(8,128)S(1)}, f32[384,256]{1,0:T(8,128)S(1)}, u32[]{:S(2)}, u32[]{:S(2)}) %collective-permute-start.2) | collective-permute-done | bytes 393248 | tf_op jit(solution)/shard_map/ppermute | solution.py:276
  124.1 3.2 %collective-permute-done.3 = f32[384,256]{1,0:T(8,128)S(1)} collective-permute-done((f32[384,256]{1,0:T(8,128)S(1)}, f32[384,256]{1,0:T(8,128)S(1)}, u32[]{:S(2)}, u32[]{:S(2)}) %collective-permute-start.3) | collective-permute-done | bytes 393248 | tf_op jit(solution)/shard_map/ppermute | solution.py:275
  127.3 0.1 slice_add_fusion.6
  127.4 5.4 %collective-permute-start.4 = (f32[256,256]{1,0:T(8,128)S(1)}, f32[256,256]{1,0:T(8,128)S(1)}, u32[]{:S(2)}, u32[]{:S(2)}) collective-permute-start(f32[256,256]{1,0:T(8,128)S(1)} %pad_maximum_fusion), channel_id=1, source_target_pairs={{0,128},{64,192},{128,0},{192,64},{1,129},{65,193},{129,1},{193,65... | collective-permute-start | bytes 786440 | tf_op jit(solution)/shard_map/ppermute | solution.py:289
  132.9 1.9 %collective-permute-start.6 = (f32[256,256]{1,0:T(8,128)S(1)}, f32[256,256]{1,0:T(8,128)S(1)}, u32[]{:S(2)}, u32[]{:S(2)}) collective-permute-start(f32[256,256]{1,0:T(8,128)S(1)} %pad_maximum_fusion.2), channel_id=1, source_target_pairs={{0,192},{64,0},{128,64},{192,128},{1,193},{65,1},{129,65},{193,129... | collective-permute-start | bytes 786440 | tf_op jit(solution)/shard_map/ppermute | solution.py:289
  134.8 5.2 %collective-permute-start.5 = (f32[256,256]{1,0:T(8,128)S(1)}, f32[256,256]{1,0:T(8,128)S(1)}, u32[]{:S(2)}, u32[]{:S(2)}) collective-permute-start(f32[256,256]{1,0:T(8,128)S(1)} %pad_maximum_fusion.1), channel_id=1, source_target_pairs={{0,64},{64,128},{128,192},{192,0},{1,65},{65,129},{129,193},{193,1... | collective-permute-start | bytes 786440 | tf_op jit(solution)/shard_map/ppermute | solution.py:289
  140.1 6.2 %collective-permute-done.4 = f32[256,256]{1,0:T(8,128)S(1)} collective-permute-done((f32[256,256]{1,0:T(8,128)S(1)}, f32[256,256]{1,0:T(8,128)S(1)}, u32[]{:S(2)}, u32[]{:S(2)}) %collective-permute-start.4) | collective-permute-done | bytes 262176 | tf_op jit(solution)/shard_map/ppermute | solution.py:289
  146.3 3.7 %collective-permute-done.6 = f32[256,256]{1,0:T(8,128)S(1)} collective-permute-done((f32[256,256]{1,0:T(8,128)S(1)}, f32[256,256]{1,0:T(8,128)S(1)}, u32[]{:S(2)}, u32[]{:S(2)}) %collective-permute-start.6) | collective-permute-done | bytes 262176 | tf_op jit(solution)/shard_map/ppermute | solution.py:289
  150.0 1.6 %collective-permute-done.5 = f32[256,256]{1,0:T(8,128)S(1)} collective-permute-done((f32[256,256]{1,0:T(8,128)S(1)}, f32[256,256]{1,0:T(8,128)S(1)}, u32[]{:S(2)}, u32[]{:S(2)}) %collective-permute-start.5) | collective-permute-done | bytes 262176 | tf_op jit(solution)/shard_map/ppermute | solution.py:289
  151.6 0.8 add_convert_fusion
  (22 shorter events, 0.3 us)
Async XLA Ops:
  67.5 26.7 %all-to-all-start.1 = ((bf16[16,400,128]{2,1,0:T(8,128)(2,1)}), bf16[16,400,128]{2,1,0:T(8,128)(2,1)S(1)}, u32[]{:S(2)}, u32[]{:S(2)}) async-start(bf16[16,400,128]{2,1,0:T(8,128)(2,1)} %get-tuple-element.28), calls=%async_computation.1 | async-start | bytes 3276800 | tf_op jit(solution)/shard_map/all_to_all | solution.py:261
  90.6 19.7 %collective-permute-start = (f32[768,256]{1,0:T(8,128)}, f32[768,256]{1,0:T(8,128)S(1)}, u32[]{:S(2)}, u32[]{:S(2)}) collective-permute-start(f32[768,256]{1,0:T(8,128)} %get-tuple-element.24), channel_id=1, source_target_pairs={{0,1},{1,2},{2,3},{3,0},{4,5},{5,6},{6,7},{7,4},{8,9},{9,10},{10,1... | collective-permute-start | bytes 2359304 | tf_op jit(solution)/shard_map/ppermute | solution.py:268
  92.3 18.1 %collective-permute-start.1 = (f32[768,256]{1,0:T(8,128)}, f32[768,256]{1,0:T(8,128)S(1)}, u32[]{:S(2)}, u32[]{:S(2)}) collective-permute-start(f32[768,256]{1,0:T(8,128)} %get-tuple-element.27), channel_id=1, source_target_pairs={{0,3},{1,0},{2,1},{3,2},{4,7},{5,4},{6,5},{7,6},{8,11},{9,8},{10,9... | collective-permute-start | bytes 2359304 | tf_op jit(solution)/shard_map/ppermute | solution.py:269
  94.2 1.2 copy-start
  95.4 14.9 %copy-start.4 = (f32[384,256]{1,0:T(8,128)S(1)}, f32[384,256]{1,0:T(8,128)}, u32[]{:S(2)}) copy-start(f32[384,256]{1,0:T(8,128)} %get-tuple-element.25) | copy-start | bytes 1179652
  95.4 14.9 %copy-start.3 = (f32[384,256]{1,0:T(8,128)S(1)}, f32[384,256]{1,0:T(8,128)}, u32[]{:S(2)}) copy-start(f32[384,256]{1,0:T(8,128)} %get-tuple-element.26) | copy-start | bytes 1179652
  95.4 28.6 %copy-start.2 = (f32[384,256]{1,0:T(8,128)S(1)}, f32[384,256]{1,0:T(8,128)}, u32[]{:S(2)}) copy-start(f32[384,256]{1,0:T(8,128)} %get-tuple-element.23) | copy-start | bytes 1179652
  95.4 31.9 %copy-start.1 = (f32[384,256]{1,0:T(8,128)S(1)}, f32[384,256]{1,0:T(8,128)}, u32[]{:S(2)}) copy-start(f32[384,256]{1,0:T(8,128)} %get-tuple-element.33) | copy-start | bytes 1179652
  104.2 47.4 %copy-start.5 = (f32[256,256]{1,0:T(8,128)S(1)}, f32[256,256]{1,0:T(8,128)}, u32[]{:S(2)}) copy-start(f32[256,256]{1,0:T(8,128)} %get-tuple-element.35) | copy-start | bytes 786436
  110.4 13.6 %collective-permute-start.2 = (f32[384,256]{1,0:T(8,128)S(1)}, f32[384,256]{1,0:T(8,128)S(1)}, u32[]{:S(2)}, u32[]{:S(2)}) collective-permute-start(f32[384,256]{1,0:T(8,128)S(1)} %slice_add_fusion), channel_id=1, source_target_pairs={{0,3},{1,0},{2,1},{3,2},{4,7},{5,4},{6,5},{7,6},{8,11},{9,8},{10,9... | collective-permute-start | bytes 1179656 | tf_op jit(solution)/shard_map/ppermute | solution.py:276
  113.5 13.8 %collective-permute-start.3 = (f32[384,256]{1,0:T(8,128)S(1)}, f32[384,256]{1,0:T(8,128)S(1)}, u32[]{:S(2)}, u32[]{:S(2)}) collective-permute-start(f32[384,256]{1,0:T(8,128)S(1)} %slice_add_fusion.1), channel_id=1, source_target_pairs={{0,1},{1,2},{2,3},{3,0},{4,5},{5,6},{6,7},{7,4},{8,9},{9,10},{10,1... | collective-permute-start | bytes 1179656 | tf_op jit(solution)/shard_map/ppermute | solution.py:275
  113.5 21.3 %collective-permute-start.7 = (f32[256,256]{1,0:T(8,128)}, f32[256,256]{1,0:T(8,128)S(1)}, u32[]{:S(2)}, u32[]{:S(2)}) collective-permute-start(f32[256,256]{1,0:T(8,128)} %get-tuple-element.36), channel_id=1, source_target_pairs={{0,1},{1,2},{2,3},{3,0},{4,5},{5,6},{6,7},{7,4},{8,9},{9,10},{10,1... | collective-permute-start | bytes 786440 | tf_op jit(solution)/shard_map/ppermute | solution.py:298
  113.6 26.5 %collective-permute-start.8 = (f32[256,256]{1,0:T(8,128)}, f32[256,256]{1,0:T(8,128)S(1)}, u32[]{:S(2)}, u32[]{:S(2)}) collective-permute-start(f32[256,256]{1,0:T(8,128)} %get-tuple-element.37), channel_id=1, source_target_pairs={{0,3},{1,0},{2,1},{3,2},{4,7},{5,4},{6,5},{7,6},{8,11},{9,8},{10,9... | collective-permute-start | bytes 786440 | tf_op jit(solution)/shard_map/ppermute | solution.py:298
  116.8 23.3 %collective-permute-start.9 = (f32[256,256]{1,0:T(8,128)}, f32[256,256]{1,0:T(8,128)S(1)}, u32[]{:S(2)}, u32[]{:S(2)}) collective-permute-start(f32[256,256]{1,0:T(8,128)} %get-tuple-element.38), channel_id=1, source_target_pairs={{0,2},{1,3},{2,0},{3,1},{4,6},{5,7},{6,4},{7,5},{8,10},{9,11},{10,... | collective-permute-start | bytes 786440 | tf_op jit(solution)/shard_map/ppermute | solution.py:299
  127.4 18.8 %collective-permute-start.4 = (f32[256,256]{1,0:T(8,128)S(1)}, f32[256,256]{1,0:T(8,128)S(1)}, u32[]{:S(2)}, u32[]{:S(2)}) collective-permute-start(f32[256,256]{1,0:T(8,128)S(1)} %pad_maximum_fusion), channel_id=1, source_target_pairs={{0,128},{64,192},{128,0},{192,64},{1,129},{65,193},{129,1},{193,65... | collective-permute-start | bytes 786440 | tf_op jit(solution)/shard_map/ppermute | solution.py:289
  132.9 17.1 %collective-permute-start.6 = (f32[256,256]{1,0:T(8,128)S(1)}, f32[256,256]{1,0:T(8,128)S(1)}, u32[]{:S(2)}, u32[]{:S(2)}) collective-permute-start(f32[256,256]{1,0:T(8,128)S(1)} %pad_maximum_fusion.2), channel_id=1, source_target_pairs={{0,192},{64,0},{128,64},{192,128},{1,193},{65,1},{129,65},{193,129... | collective-permute-start | bytes 786440 | tf_op jit(solution)/shard_map/ppermute | solution.py:289
  134.8 16.8 %collective-permute-start.5 = (f32[256,256]{1,0:T(8,128)S(1)}, f32[256,256]{1,0:T(8,128)S(1)}, u32[]{:S(2)}, u32[]{:S(2)}) collective-permute-start(f32[256,256]{1,0:T(8,128)S(1)} %pad_maximum_fusion.1), channel_id=1, source_target_pairs={{0,64},{64,128},{128,192},{192,0},{1,65},{65,129},{129,193},{193,1... | collective-permute-start | bytes 786440 | tf_op jit(solution)/shard_map/ppermute | solution.py:289

commit v4 on v3

--- a/solution.py
+++ b/solution.py
@@ -13,6 +13,7 @@
 META = 16
 DEPTH = 4
 WIDE = 4
+PARTS = 4
 ORDER = (2, 1, 3, 0)
 CHUNKS = (3, 1)
 FIRST = (0, 3)
@@ -28,14 +29,22 @@
 
 def route_kernel(kc, jb, owner, tiles, *rest):
     sends, scratch = rest[: len(CHUNKS)], rest[len(CHUNKS) :]
-    kc_s, jb_s, owner_s, counts, codes, kind_sem, sem = scratch
+    kc_s, jb_s, owner_s, counts, codes, metas, stage, kind_sem, stage_sem, meta_sem, sem = scratch
     held = tiles.shape[0]
+    part = held // PARTS
+
+    def load_part(p):
+        some = pl.ds(p * part, part)
+        return pltpu.make_async_copy(tiles.at[some], stage.at[some], stage_sem.at[p])
+
     loads = [
         pltpu.make_async_copy(a, b, kind_sem.at[i])
         for i, (a, b) in enumerate(((kc, kc_s), (jb, jb_s), (owner, owner_s)))
     ]
     for load in loads:
         load.start()
+    for p in range(PARTS):
+        load_part(p).start()
 
     def clear(o, carry):
         counts[o] = 0
@@ -62,22 +71,29 @@
             @pl.when((step >= FIRST[c]) & (step < FIRST[c] + CHUNKS[c]))
             def _():
                 row = pl.multiple_of(((step - FIRST[c]) * CAP + rank) * TILE, TILE)
-                pltpu.make_async_copy(tiles.at[i], send.at[dest, pl.ds(row, TILE), :], sem).start()
+                pltpu.make_async_copy(stage.at[i], send.at[dest, pl.ds(row, TILE), :], sem).start()
 
         line = pl.ds(dest, 1)
         code = (kc_s[i] * 2 + jb_s[i]).astype(jnp.float32)
         codes[line, :] = jnp.where(lane == step * CAP + rank, code, codes[line, :])
         return carry
 
-    lax.fori_loop(0, held, one, 0)
+    for p in range(PARTS):
+        load_part(p).wait()
+        lax.fori_loop(p * part, (p + 1) * part, one, 0)
+    copies = []
     for c, send in enumerate(sends):
         found = codes[...]
         if FIRST[c]:
             found = pltpu.roll(found, TILE - FIRST[c] * CAP, axis=1)
-        send[:, slots_of(CHUNKS[c]) * TILE :, :] = jnp.broadcast_to(
-            found[:, None, :], (GROUP, META, TILE)
-        ).astype(send.dtype)
-    pltpu.make_async_copy(tiles, tiles, sem).wait()
+        metas[c] = jnp.broadcast_to(found[:, None, :], (GROUP, META, TILE)).astype(metas.dtype)
+        there = send.at[:, pl.ds(slots_of(CHUNKS[c]) * TILE, META), :]
+        copies.append(pltpu.make_async_copy(metas.at[c], there, meta_sem.at[c]))
+    for copy in copies:
+        copy.start()
+    for copy in copies:
+        copy.wait()
+    pltpu.make_async_copy(stage, stage, sem).wait()
 
 
 def route(kc, jb, owner, tiles):
@@ -87,14 +103,18 @@
         route_kernel,
         out_shape=[jax.ShapeDtypeStruct((GROUP, block_of(n), TILE), tiles.dtype) for n in CHUNKS],
         in_specs=[hbm] * 4,
-        out_specs=[pl.BlockSpec(memory_space=pltpu.VMEM)] * len(CHUNKS),
+        out_specs=[hbm] * len(CHUNKS),
         scratch_shapes=[
             pltpu.SMEM((held,), jnp.int32),
             pltpu.SMEM((held,), jnp.int32),
             pltpu.SMEM((held,), jnp.int32),
             pltpu.SMEM((HIGH * GROUP,), jnp.int32),
             pltpu.VMEM((GROUP, TILE), jnp.float32),
+            pltpu.VMEM((len(CHUNKS), GROUP, META, TILE), tiles.dtype),
+            pltpu.VMEM(tiles.shape, tiles.dtype),
             pltpu.SemaphoreType.DMA((3,)),
+            pltpu.SemaphoreType.DMA((PARTS,)),
+            pltpu.SemaphoreType.DMA((len(CHUNKS),)),
             pltpu.SemaphoreType.DMA,
         ],
         compiler_params=pltpu.CompilerParams(vmem_limit_bytes=60 << 20),
@@ -106,86 +126,86 @@
 def contract_kernel(steps, direct, got, w, *rest):
     many = 4 if direct else 6
     outs = rest[:many]
-    tiles, total, held, codes_b, codes_v, codes, rows, cols, sums, sems, w_sem = rest[many:]
+    tiles, total, held, codes_b, codes_v, codes, work, sems, w_sem = rest[many:]
     row_count = w.shape[0]
     half = row_count // X // 2
-    slots = slots_of(steps)
-    zero = GROUP * slots
+    deep = CAP * TILE
     metas = pltpu.make_async_copy(got.at[:, pl.ds(got.shape[1] - META, META), :], codes_b, sems.at[0])
     metas.start()
-    arrives = []
-    for j in range(GROUP):
-        arrives.append(
-            pltpu.make_async_copy(
-                got.at[j, pl.ds(0, slots * TILE), :],
-                tiles.at[pl.ds(j * slots * TILE, slots * TILE), :],
-                sems.at[2 + j],
-            )
-        )
-    for arrive in arrives:
-        arrive.start()
-    tiles[zero * TILE :, :] = jnp.zeros((TILE, TILE), tiles.dtype)
+
+    def arrive(s):
+        here = got.at[:, pl.ds(s * deep, deep), :]
+        return pltpu.make_async_copy(here, tiles.at[pl.ds(s * GROUP, GROUP)], sems.at[2 + s])
+
+    for s in range(steps):
+        arrive(s).start()
+    tiles[steps * GROUP] = jnp.zeros((deep, TILE), tiles.dtype)
     metas.wait()
     codes_v[...] = codes_b[...][:, 0, :].astype(jnp.float32).astype(jnp.int32)
     copy = pltpu.make_async_copy(codes_v, codes, sems.at[1])
     copy.start()
     total[...] = jnp.zeros_like(total)
     copy.wait()
-    count = jnp.int32(0)
-    for which in range(2 * steps):
-        for j in range(GROUP):
-            for rank in range(CAP):
-                slot = which // 2 * CAP + rank
-                code = codes[j, slot]
-                rows[count] = (j * slots + slot) * TILE
-                cols[count] = lax.shift_right_arithmetic(code, 1) * TILE
-                sums[count] = which
-                count = count + jnp.where((code >= 0) & ((code & 1) == which % 2), 1, 0)
-        for _ in range(WIDE - 1):
-            rows[count] = zero * TILE
-            cols[count] = 0
-            sums[count] = which
-            count = count + jnp.where(lax.rem(count, WIDE) > 0, 1, 0)
-    bunches = lax.div(count, WIDE)
 
     def fetch(i, b, side):
-        start = pl.multiple_of(cols[WIDE * i + side], TILE)
+        start = pl.multiple_of(lax.shift_right_logical(work[WIDE * i + side], 10) * TILE, TILE)
         return pltpu.make_async_copy(
             w.at[:, pl.ds(start, TILE)],
             held.at[b, :, pl.ds(side * TILE, TILE)],
             w_sem.at[b, side],
         )
 
-    for b in range(DEPTH):
-
-        @pl.when(b < bunches)
-        def _():
+    def fetch_first(least, most):
+        for b in range(DEPTH):
+
+            @pl.when((b >= least) & (b < most))
+            def _():
+                for side in range(WIDE):
+                    fetch(b, b, side).start()
+
+    count = jnp.int32(0)
+    bounds = [jnp.int32(0)]
+    for which in range(2 * steps):
+        for j in range(GROUP):
+            for rank in range(CAP):
+                code = codes[j, which // 2 * CAP + rank]
+                place = (which // 2 * GROUP + j) * 4 + rank
+                work[count] = lax.shift_left(lax.shift_right_arithmetic(code, 1), 10) + place
+                count = count + jnp.where((code >= 0) & ((code & 1) == which % 2), 1, 0)
+        for _ in range(WIDE - 1):
+            work[count] = steps * GROUP * 4
+            count = count + jnp.where(lax.rem(count, WIDE) > 0, 1, 0)
+        bounds.append(lax.div(count, WIDE))
+        if which == 1:
+            fetch_first(0, bounds[2])
+    bunches = bounds[-1]
+    if steps > 1:
+        fetch_first(bounds[2], bunches)
+
+    def picked(i, side):
+        place = work[WIDE * i + side] & 1023
+        row = pl.multiple_of((place & 3) * TILE, TILE)
+        return tiles[lax.shift_right_logical(place, 2), pl.ds(row, TILE), :]
+
+    for s in range(steps):
+        arrive(s).wait()
+
+        def one(i, carry, s=s):
+            b = lax.rem(i, DEPTH)
             for side in range(WIDE):
-                fetch(b, b, side).start()
-
-    for arrive in arrives:
-        arrive.wait()
-
-    def one(i, carry):
-        b = lax.rem(i, DEPTH)
-        for side in range(WIDE):
-            fetch(i, b, side).wait()
-        picked = [
-            tiles[pl.ds(pl.multiple_of(rows[WIDE * i + side], TILE), TILE), :]
-            for side in range(WIDE)
-        ]
-        total[sums[WIDE * i]] += jnp.dot(
-            held[b], jnp.concatenate(picked, axis=0), preferred_element_type=jnp.float32
-        )
-
-        @pl.when(i + DEPTH < bunches)
-        def _():
-            for side in range(WIDE):
-                fetch(i + DEPTH, b, side).start()
-
-        return carry
-
-    lax.fori_loop(0, bunches, one, 0)
+                fetch(i, b, side).wait()
+            right = jnp.concatenate([picked(i, side) for side in range(WIDE)], axis=0)
+            which = 2 * s + jnp.where(i >= bounds[2 * s + 1], 1, 0)
+            total[which] += jnp.dot(held[b], right, preferred_element_type=jnp.float32)
+
+            @pl.when(i + DEPTH < bunches)
+            def _():
+                for side in range(WIDE):
+                    fetch(i + DEPTH, b, side).start()
+
+            return carry
+
+        lax.fori_loop(bounds[2 * s], bounds[2 * s + 2], one, 0)
     x = lax.axis_index("x")
 
     def give(ref, at, away, side):
@@ -234,16 +254,14 @@
         in_specs=[hbm, hbm],
         out_specs=[vmem] * len(outs),
         scratch_shapes=[
-            pltpu.VMEM(((GROUP * slots + 1) * TILE, TILE), jnp.bfloat16),
+            pltpu.VMEM((steps * GROUP + 1, CAP * TILE, TILE), jnp.bfloat16),
             pltpu.VMEM((2 * steps, row_count, TILE), jnp.float32),
             pltpu.VMEM((DEPTH, row_count, WIDE * TILE), jnp.bfloat16),
             pltpu.VMEM((GROUP, META, TILE), jnp.bfloat16),
             pltpu.VMEM((GROUP, TILE), jnp.int32),
             pltpu.SMEM((GROUP, TILE), jnp.int32),
             pltpu.SMEM((most,), jnp.int32),
-            pltpu.SMEM((most,), jnp.int32),
-            pltpu.SMEM((most,), jnp.int32),
-            pltpu.SemaphoreType.DMA((2 + GROUP,)),
+            pltpu.SemaphoreType.DMA((2 + steps,)),
             pltpu.SemaphoreType.DMA((DEPTH, WIDE)),
         ],
         compiler_params=pltpu.CompilerParams(vmem_limit_bytes=56 << 20),

time: 155 us -> 152 us (0.981)
  waiting for transfers between devices: 27 us -> 34.3 us
  Pallas kernels: 32.8 us -> 27.2 us
  starting transfers between devices: 28.6 us -> 24.4 us
    pallas_call x2, Pallas kernels: 26.8 us -> 23.6 us  [contract(): pl.pallas_call(kernel, out_shape=outs, in_specs=[hbm, hbm], out_specs=[vm...]
    ppermute x3, starting transfers between devices: 12.6 us -> 9.48 us  [send(): lax.ppermute(block, 'zh', [(i, (i + away) % HIGH) for i in range(HIGH)])]
    ppermute x3, waiting for transfers between devices: 11.5 us -> 14.5 us  [send(): lax.ppermute(block, 'zh', [(i, (i + away) % HIGH) for i in range(HIGH)])]
    all_to_all x1, waiting for transfers between devices: 0.35 us -> 3.36 us  [local(): lax.all_to_all(sent, ('zl', 'y', 'k'), split_axis=0, concat_axis=0, tiled...]
    pallas_call x1, Pallas kernels: 5.99 us -> 3.54 us  [route(): pl.pallas_call(route_kernel, out_shape=[jax.ShapeDtypeStruct((GROUP, bloc...]
    ppermute x1, waiting for transfers between devices: 0.01 us -> 2.38 us  [local(): lax.ppermute(after, 'x', up_x)]
    ppermute x1, waiting for transfers between devices: 6.13 us -> 3.94 us  [join(): from_low = lax.ppermute(up, 'x', up_x)]
    ppermute x1, waiting for transfers between devices: 0.01 us -> 1.7 us  [join(): from_high = lax.ppermute(down, 'x', down_x)]
  transfers between devices with their start and end apart: 11 -> 11, of which waited for: 7 -> 8; matrix products, arithmetic and copies ran while one was open for 0% -> 0% of each run, Pallas kernels for 18% -> 16%
where the time goes in v4:
time: 152 us; the launch traced here: 150 us
  blocking collectives  61.5 us (40%)
  waiting for transfers between devices  34.3 us (23%)
  Pallas kernels  27.2 us (18%)
  starting transfers between devices  24.4 us (16%)
    all_to_all x1, blocking collectives, local(): lax.all_to_all(sent, ('zl', 'y', 'k'), split_axis=0, concat_axis=0, tiled...  61.5 us
    pallas_call x2, Pallas kernels, contract(): pl.pallas_call(kernel, out_shape=outs, in_specs=[hbm, hbm], out_specs=[vm...  23.6 us
    ppermute x3, waiting for transfers between devices, send(): lax.ppermute(block, 'zh', [(i, (i + away) % HIGH) for i in range(HIGH)])  14.5 us
    ppermute x3, starting transfers between devices, send(): lax.ppermute(block, 'zh', [(i, (i + away) % HIGH) for i in range(HIGH)])  9.48 us
    ppermute x1, waiting for transfers between devices, blocks(): from_high_a = lax.ppermute(last_a, 'x', down_x)  5.41 us
    all_to_all x1, starting transfers between devices, local(): lax.all_to_all(sent, ('zl', 'y', 'k'), split_axis=0, concat_axis=0, tiled...  4.99 us
    ppermute x1, waiting for transfers between devices, join(): from_low = lax.ppermute(up, 'x', up_x)  3.94 us
    pallas_call x1, Pallas kernels, route(): pl.pallas_call(route_kernel, out_shape=[jax.ShapeDtypeStruct((GROUP, bloc...  3.54 us
  transfers between devices with their start and end apart: 11, of which 8 were waited for; matrix products, arithmetic and copies ran while one was open for 0% of the time, Pallas kernels for 16%

profile of v4, /device:TPU:32, one launch (start us, length us, event | category | flops | bytes accessed | tf_op | source)
XLA Modules:
  0.0 149.7 jit_solution(8117933171665072885)
XLA Ops:
  0.0 3.5 %route.1 = (bf16[16,1168,128]{2,1,0:T(8,128)(2,1)}, bf16[16,400,128]{2,1,0:T(8,128)(2,1)}) custom-call(s32[96]{0:T(128)} %kc.1, s32[96]{0:T(128)} %jb.1, s32[96]{0:T(128)} %bitcast.1, bf16[96,128,128]{2,1,0:T(8,128)(2,1)} %tiles.1), custom_call_target="tpu_custom_call" | custom-call | bytes 8388608 | tf_op jit(solution)/shard_map/route/pallas_call | solution.py:102
  3.5 61.5 %all_to_all.10.refs_0_ = bf16[16,1168,128]{2,1,0:T(8,128)(2,1)} all-to-all(bf16[16,1168,128]{2,1,0:T(8,128)(2,1)} %get-tuple-element.22), channel_id=1, replica_groups=mesh['zh'=4,'zl'=2,'y'=4,'k'=2,'x'=4] {'zl','y','k'}, dimensions={0} | all-to-all | bytes 9568256 | tf_op jit(solution)/shard_map/all_to_all | solution.py:279
  65.0 5.0 %all-to-all-start.1 = ((bf16[16,400,128]{2,1,0:T(8,128)(2,1)}), bf16[16,400,128]{2,1,0:T(8,128)(2,1)S(1)}, u32[]{:S(2)}, u32[]{:S(2)}) async-start(bf16[16,400,128]{2,1,0:T(8,128)(2,1)} %get-tuple-element.28), calls=%async_computation.1 | async-start | bytes 3276800 | tf_op jit(solution)/shard_map/all_to_all | solution.py:279
  70.0 15.1 %contract.2 = (f32[384,256]{1,0:T(8,128)}, f32[384,256]{1,0:T(8,128)}, f32[768,256]{1,0:T(8,128)}, f32[768,256]{1,0:T(8,128)}, f32[384,256]{1,0:T(8,128)}, /*index=5*/f32[384,256]{1,0:T(8,128)}) custom-call(bf16[16,1168,128]{2,1,0:T(8,128)(2,1)} %all_to_all.10.refs_0_, bf16[1024,8192]{1,0:T(8,128)(2,1)} %refs_1_.3), custom_call_target="tpu_custom_call" | custom-call | flops 1048576 | bytes 1048576 | tf_op jit(solution)/shard_map/contract/pallas_call | solution.py:251
  85.1 2.2 %collective-permute-start = (f32[768,256]{1,0:T(8,128)}, f32[768,256]{1,0:T(8,128)S(1)}, u32[]{:S(2)}, u32[]{:S(2)}) collective-permute-start(f32[768,256]{1,0:T(8,128)} %get-tuple-element.24), channel_id=1, source_target_pairs={{0,1},{1,2},{2,3},{3,0},{4,5},{5,6},{6,7},{7,4},{8,9},{9,10},{10,1... | collective-permute-start | bytes 2359304 | tf_op jit(solution)/shard_map/ppermute | solution.py:286
  87.3 1.1 collective-permute-start.1
  88.4 3.4 %all-to-all-done.1.refs_0_ = bf16[16,400,128]{2,1,0:T(8,128)(2,1)S(1)} async-done(((bf16[16,400,128]{2,1,0:T(8,128)(2,1)}), bf16[16,400,128]{2,1,0:T(8,128)(2,1)S(1)}, u32[]{:S(2)}, u32[]{:S(2)}) %all-to-all-start.1) | async-done | bytes 1638432 | tf_op jit(solution)/shard_map/all_to_all | solution.py:279
  91.8 1.2 copy-done
  93.0 8.6 %contract.3 = (f32[256,256]{1,0:T(8,128)}, f32[256,256]{1,0:T(8,128)}, f32[256,256]{1,0:T(8,128)}, f32[256,256]{1,0:T(8,128)}) custom-call(bf16[16,400,128]{2,1,0:T(8,128)(2,1)} %copy-done, bf16[1024,8192]{1,0:T(8,128)(2,1)} %refs_1_.3), custom_call_target="tpu_custom_call" | custom-call | flops 1048576 | bytes 1048576 | tf_op jit(solution)/shard_map/contract/pallas_call | solution.py:251
  101.6 3.9 %collective-permute-done = f32[768,256]{1,0:T(8,128)S(1)} collective-permute-done((f32[768,256]{1,0:T(8,128)}, f32[768,256]{1,0:T(8,128)S(1)}, u32[]{:S(2)}, u32[]{:S(2)}) %collective-permute-start) | collective-permute-done | bytes 786464 | tf_op jit(solution)/shard_map/ppermute | solution.py:286
  105.6 1.7 %collective-permute-done.1 = f32[768,256]{1,0:T(8,128)S(1)} collective-permute-done((f32[768,256]{1,0:T(8,128)}, f32[768,256]{1,0:T(8,128)S(1)}, u32[]{:S(2)}, u32[]{:S(2)}) %collective-permute-start.1) | collective-permute-done | bytes 786464 | tf_op jit(solution)/shard_map/ppermute | solution.py:287
  107.3 1.9 %collective-permute-start.2 = (f32[384,256]{1,0:T(8,128)S(1)}, f32[384,256]{1,0:T(8,128)S(1)}, u32[]{:S(2)}, u32[]{:S(2)}) collective-permute-start(f32[384,256]{1,0:T(8,128)S(1)} %slice_add_fusion), channel_id=1, source_target_pairs={{0,3},{1,0},{2,1},{3,2},{4,7},{5,4},{6,5},{7,6},{8,11},{9,8},{10,9... | collective-permute-start | bytes 1179656 | tf_op jit(solution)/shard_map/ppermute | solution.py:294
  109.4 0.5 collective-permute-start.7
  110.0 2.7 %collective-permute-start.8 = (f32[256,256]{1,0:T(8,128)}, f32[256,256]{1,0:T(8,128)S(1)}, u32[]{:S(2)}, u32[]{:S(2)}) collective-permute-start(f32[256,256]{1,0:T(8,128)} %get-tuple-element.37), channel_id=1, source_target_pairs={{0,3},{1,0},{2,1},{3,2},{4,7},{5,4},{6,5},{7,6},{8,11},{9,8},{10,9... | collective-permute-start | bytes 786440 | tf_op jit(solution)/shard_map/ppermute | solution.py:316
  112.7 1.2 collective-permute-start.9
  113.9 5.4 %collective-permute-done.2 = f32[384,256]{1,0:T(8,128)S(1)} collective-permute-done((f32[384,256]{1,0:T(8,128)S(1)}, f32[384,256]{1,0:T(8,128)S(1)}, u32[]{:S(2)}, u32[]{:S(2)}) %collective-permute-start.2) | collective-permute-done | bytes 393248 | tf_op jit(solution)/shard_map/ppermute | solution.py:294
  119.4 3.0 %collective-permute-done.3 = f32[384,256]{1,0:T(8,128)S(1)} collective-permute-done((f32[384,256]{1,0:T(8,128)S(1)}, f32[384,256]{1,0:T(8,128)S(1)}, u32[]{:S(2)}, u32[]{:S(2)}) %collective-permute-start.3) | collective-permute-done | bytes 393248 | tf_op jit(solution)/shard_map/ppermute | solution.py:293
  122.5 7.3 %collective-permute-start.4 = (f32[256,256]{1,0:T(8,128)S(1)}, f32[256,256]{1,0:T(8,128)S(1)}, u32[]{:S(2)}, u32[]{:S(2)}) collective-permute-start(f32[256,256]{1,0:T(8,128)S(1)} %pad_maximum_fusion), channel_id=1, source_target_pairs={{0,128},{64,192},{128,0},{192,64},{1,129},{65,193},{129,1},{193,65... | collective-permute-start | bytes 786440 | tf_op jit(solution)/shard_map/ppermute | solution.py:307
  129.8 1.2 collective-permute-start.6
  131.0 2.4 %collective-permute-done.7 = f32[256,256]{1,0:T(8,128)S(1)} collective-permute-done((f32[256,256]{1,0:T(8,128)}, f32[256,256]{1,0:T(8,128)S(1)}, u32[]{:S(2)}, u32[]{:S(2)}) %collective-permute-start.7) | collective-permute-done | bytes 262176 | tf_op jit(solution)/shard_map/ppermute | solution.py:316
  133.4 1.0 collective-permute-start.5
  134.4 9.6 %collective-permute-done.4 = f32[256,256]{1,0:T(8,128)S(1)} collective-permute-done((f32[256,256]{1,0:T(8,128)S(1)}, f32[256,256]{1,0:T(8,128)S(1)}, u32[]{:S(2)}, u32[]{:S(2)}) %collective-permute-start.4) | collective-permute-done | bytes 262176 | tf_op jit(solution)/shard_map/ppermute | solution.py:307
  144.1 4.9 %collective-permute-done.6 = f32[256,256]{1,0:T(8,128)S(1)} collective-permute-done((f32[256,256]{1,0:T(8,128)S(1)}, f32[256,256]{1,0:T(8,128)S(1)}, u32[]{:S(2)}, u32[]{:S(2)}) %collective-permute-start.6) | collective-permute-done | bytes 262176 | tf_op jit(solution)/shard_map/ppermute | solution.py:307
  149.0 0.8 add_convert_fusion
  (22 shorter events, 0.6 us)
Async XLA Ops:
  65.0 26.7 %all-to-all-start.1 = ((bf16[16,400,128]{2,1,0:T(8,128)(2,1)}), bf16[16,400,128]{2,1,0:T(8,128)(2,1)S(1)}, u32[]{:S(2)}, u32[]{:S(2)}) async-start(bf16[16,400,128]{2,1,0:T(8,128)(2,1)} %get-tuple-element.28), calls=%async_computation.1 | async-start | bytes 3276800 | tf_op jit(solution)/shard_map/all_to_all | solution.py:279
  85.1 20.4 %collective-permute-start = (f32[768,256]{1,0:T(8,128)}, f32[768,256]{1,0:T(8,128)S(1)}, u32[]{:S(2)}, u32[]{:S(2)}) collective-permute-start(f32[768,256]{1,0:T(8,128)} %get-tuple-element.24), channel_id=1, source_target_pairs={{0,1},{1,2},{2,3},{3,0},{4,5},{5,6},{6,7},{7,4},{8,9},{9,10},{10,1... | collective-permute-start | bytes 2359304 | tf_op jit(solution)/shard_map/ppermute | solution.py:286
  87.3 20.0 %collective-permute-start.1 = (f32[768,256]{1,0:T(8,128)}, f32[768,256]{1,0:T(8,128)S(1)}, u32[]{:S(2)}, u32[]{:S(2)}) collective-permute-start(f32[768,256]{1,0:T(8,128)} %get-tuple-element.27), channel_id=1, source_target_pairs={{0,3},{1,0},{2,1},{3,2},{4,7},{5,4},{6,5},{7,6},{8,11},{9,8},{10,9... | collective-permute-start | bytes 2359304 | tf_op jit(solution)/shard_map/ppermute | solution.py:287
  91.8 1.2 copy-start
  93.0 12.5 %copy-start.4 = (f32[384,256]{1,0:T(8,128)S(1)}, f32[384,256]{1,0:T(8,128)}, u32[]{:S(2)}) copy-start(f32[384,256]{1,0:T(8,128)} %get-tuple-element.25) | copy-start | bytes 1179652
  93.0 14.3 %copy-start.3 = (f32[384,256]{1,0:T(8,128)S(1)}, f32[384,256]{1,0:T(8,128)}, u32[]{:S(2)}) copy-start(f32[384,256]{1,0:T(8,128)} %get-tuple-element.26) | copy-start | bytes 1179652
  93.0 26.4 %copy-start.2 = (f32[384,256]{1,0:T(8,128)S(1)}, f32[384,256]{1,0:T(8,128)}, u32[]{:S(2)}) copy-start(f32[384,256]{1,0:T(8,128)} %get-tuple-element.23) | copy-start | bytes 1179652
  93.0 29.4 %copy-start.1 = (f32[384,256]{1,0:T(8,128)S(1)}, f32[384,256]{1,0:T(8,128)}, u32[]{:S(2)}) copy-start(f32[384,256]{1,0:T(8,128)} %get-tuple-element.33) | copy-start | bytes 1179652
  101.6 47.4 %copy-start.5 = (f32[256,256]{1,0:T(8,128)S(1)}, f32[256,256]{1,0:T(8,128)}, u32[]{:S(2)}) copy-start(f32[256,256]{1,0:T(8,128)} %get-tuple-element.35) | copy-start | bytes 786436
  107.3 12.0 %collective-permute-start.2 = (f32[384,256]{1,0:T(8,128)S(1)}, f32[384,256]{1,0:T(8,128)S(1)}, u32[]{:S(2)}, u32[]{:S(2)}) collective-permute-start(f32[384,256]{1,0:T(8,128)S(1)} %slice_add_fusion), channel_id=1, source_target_pairs={{0,3},{1,0},{2,1},{3,2},{4,7},{5,4},{6,5},{7,6},{8,11},{9,8},{10,9... | collective-permute-start | bytes 1179656 | tf_op jit(solution)/shard_map/ppermute | solution.py:294
  109.2 13.2 %collective-permute-start.3 = (f32[384,256]{1,0:T(8,128)S(1)}, f32[384,256]{1,0:T(8,128)S(1)}, u32[]{:S(2)}, u32[]{:S(2)}) collective-permute-start(f32[384,256]{1,0:T(8,128)S(1)} %slice_add_fusion.1), channel_id=1, source_target_pairs={{0,1},{1,2},{2,3},{3,0},{4,5},{5,6},{6,7},{7,4},{8,9},{9,10},{10,1... | collective-permute-start | bytes 1179656 | tf_op jit(solution)/shard_map/ppermute | solution.py:293
  109.4 24.0 %collective-permute-start.7 = (f32[256,256]{1,0:T(8,128)}, f32[256,256]{1,0:T(8,128)S(1)}, u32[]{:S(2)}, u32[]{:S(2)}) collective-permute-start(f32[256,256]{1,0:T(8,128)} %get-tuple-element.36), channel_id=1, source_target_pairs={{0,1},{1,2},{2,3},{3,0},{4,5},{5,6},{6,7},{7,4},{8,9},{9,10},{10,1... | collective-permute-start | bytes 786440 | tf_op jit(solution)/shard_map/ppermute | solution.py:316
  110.0 24.5 %collective-permute-start.8 = (f32[256,256]{1,0:T(8,128)}, f32[256,256]{1,0:T(8,128)S(1)}, u32[]{:S(2)}, u32[]{:S(2)}) collective-permute-start(f32[256,256]{1,0:T(8,128)} %get-tuple-element.37), channel_id=1, source_target_pairs={{0,3},{1,0},{2,1},{3,2},{4,7},{5,4},{6,5},{7,6},{8,11},{9,8},{10,9... | collective-permute-start | bytes 786440 | tf_op jit(solution)/shard_map/ppermute | solution.py:316
  112.7 21.8 %collective-permute-start.9 = (f32[256,256]{1,0:T(8,128)}, f32[256,256]{1,0:T(8,128)S(1)}, u32[]{:S(2)}, u32[]{:S(2)}) collective-permute-start(f32[256,256]{1,0:T(8,128)} %get-tuple-element.38), channel_id=1, source_target_pairs={{0,2},{1,3},{2,0},{3,1},{4,6},{5,7},{6,4},{7,5},{8,10},{9,11},{10,... | collective-permute-start | bytes 786440 | tf_op jit(solution)/shard_map/ppermute | solution.py:317
  122.5 21.5 %collective-permute-start.4 = (f32[256,256]{1,0:T(8,128)S(1)}, f32[256,256]{1,0:T(8,128)S(1)}, u32[]{:S(2)}, u32[]{:S(2)}) collective-permute-start(f32[256,256]{1,0:T(8,128)S(1)} %pad_maximum_fusion), channel_id=1, source_target_pairs={{0,128},{64,192},{128,0},{192,64},{1,129},{65,193},{129,1},{193,65... | collective-permute-start | bytes 786440 | tf_op jit(solution)/shard_map/ppermute | solution.py:307
  129.8 19.2 %collective-permute-start.6 = (f32[256,256]{1,0:T(8,128)S(1)}, f32[256,256]{1,0:T(8,128)S(1)}, u32[]{:S(2)}, u32[]{:S(2)}) collective-permute-start(f32[256,256]{1,0:T(8,128)S(1)} %pad_maximum_fusion.2), channel_id=1, source_target_pairs={{0,192},{64,0},{128,64},{192,128},{1,193},{65,1},{129,65},{193,129... | collective-permute-start | bytes 786440 | tf_op jit(solution)/shard_map/ppermute | solution.py:307
  133.4 15.6 %collective-permute-start.5 = (f32[256,256]{1,0:T(8,128)S(1)}, f32[256,256]{1,0:T(8,128)S(1)}, u32[]{:S(2)}, u32[]{:S(2)}) collective-permute-start(f32[256,256]{1,0:T(8,128)S(1)} %pad_maximum_fusion.1), channel_id=1, source_target_pairs={{0,64},{64,128},{128,192},{192,0},{1,65},{65,129},{129,193},{193,1... | collective-permute-start | bytes 786440 | tf_op jit(solution)/shard_map/ppermute | solution.py:307

commit v5 on v4

--- a/solution.py
+++ b/solution.py
@@ -309,9 +309,11 @@
     steps = CHUNKS[0]
     first = contract(steps, False, gots[0], w_slices)
     own, after, far, behind = contract(CHUNKS[1], True, gots[1], w_slices)
-    first = join(steps, first)
-    low_b, high_a, after, behind, far = lax.optimization_barrier((*first[:2], after, behind, far))
-    early = blocks(steps, (low_b, high_a, *first[2:]))
+    *first, next_b, last_a = first
+    next_b, last_a, own = lax.optimization_barrier((next_b, last_a, own))
+    first = join(steps, (*first, next_b, last_a))
+    early = blocks(steps, first)
+    after, behind, far, *early = lax.optimization_barrier((after, behind, far, *early))
     parts = [send(b, ORDER[s]) for s, b in enumerate(early)]
     parts += [own, lax.ppermute(after, "x", up_x), lax.ppermute(behind, "x", down_x)]
     parts += [lax.ppermute(far, "x", [(i, (i + 2) % X) for i in range(X)])]

time: 152 us -> 151 us (level)
  Pallas kernels: 27.2 us -> 24.4 us
  starting transfers between devices: 24.4 us -> 26.4 us
    ppermute x1, waiting for transfers between devices: 5.41 us -> 0.01 us  [blocks(): from_high_a = lax.ppermute(last_a, 'x', down_x)]
    ppermute x1, waiting for transfers between devices: 3 us -> 8.17 us  [blocks(): from_low_b = lax.ppermute(next_b, 'x', up_x)]
    pallas_call x2, Pallas kernels: 23.6 us -> 20.9 us  [contract(): pl.pallas_call(kernel, out_shape=outs, in_specs=[hbm, hbm], out_specs=[vm...]
    ppermute x3, waiting for transfers between devices: 14.5 us -> 17 us  [send(): lax.ppermute(block, 'zh', [(i, (i + away) % HIGH) for i in range(HIGH)])]
    ppermute x1, waiting for transfers between devices: 2.38 us -> 0.01 us  [local(): lax.ppermute(after, 'x', up_x)]
    ppermute x1, waiting for transfers between devices: 1.7 us -> 0.01 us  [join(): from_high = lax.ppermute(down, 'x', down_x)]
    ppermute x1, waiting for transfers between devices: 3.94 us -> 5.5 us  [join(): from_low = lax.ppermute(up, 'x', up_x)]
  transfers between devices with their start and end apart: 11 -> 11, of which waited for: 8 -> 5; matrix products, arithmetic and copies ran while one was open for 0% -> 0% of each run, Pallas kernels for 16% -> 14%
where the time goes in v5:
time: 151 us; the launch traced here: 150 us
  blocking collectives  61.5 us (41%)
  waiting for transfers between devices  34.9 us (23%)
  starting transfers between devices  26.4 us (17%)
  Pallas kernels  24.4 us (16%)
    all_to_all x1, blocking collectives, local(): lax.all_to_all(sent, ('zl', 'y', 'k'), split_axis=0, concat_axis=0, tiled...  61.5 us
    pallas_call x2, Pallas kernels, contract(): pl.pallas_call(kernel, out_shape=outs, in_specs=[hbm, hbm], out_specs=[vm...  20.9 us
    ppermute x3, waiting for transfers between devices, send(): lax.ppermute(block, 'zh', [(i, (i + away) % HIGH) for i in range(HIGH)])  17 us
    ppermute x3, starting transfers between devices, send(): lax.ppermute(block, 'zh', [(i, (i + away) % HIGH) for i in range(HIGH)])  9.78 us
    ppermute x1, waiting for transfers between devices, blocks(): from_low_b = lax.ppermute(next_b, 'x', up_x)  8.17 us
    ppermute x1, waiting for transfers between devices, join(): from_low = lax.ppermute(up, 'x', up_x)  5.5 us
    all_to_all x1, starting transfers between devices, local(): lax.all_to_all(sent, ('zl', 'y', 'k'), split_axis=0, concat_axis=0, tiled...  4.99 us
    all_to_all x1, waiting for transfers between devices, local(): lax.all_to_all(sent, ('zl', 'y', 'k'), split_axis=0, concat_axis=0, tiled...  4.26 us
  transfers between devices with their start and end apart: 11, of which 5 were waited for; matrix products, arithmetic and copies ran while one was open for 0% of the time, Pallas kernels for 14%

profile of v5, /device:TPU:32, one launch (start us, length us, event | category | flops | bytes accessed | tf_op | source)
XLA Modules:
  0.0 149.7 jit_solution(9987371636576383748)
XLA Ops:
  0.0 3.5 %route.1 = (bf16[16,1168,128]{2,1,0:T(8,128)(2,1)}, bf16[16,400,128]{2,1,0:T(8,128)(2,1)}) custom-call(s32[96]{0:T(128)} %kc.1, s32[96]{0:T(128)} %jb.1, s32[96]{0:T(128)} %bitcast.1, bf16[96,128,128]{2,1,0:T(8,128)(2,1)} %tiles.1), custom_call_target="tpu_custom_call" | custom-call | bytes 8388608 | tf_op jit(solution)/shard_map/route/pallas_call | solution.py:102
  3.5 61.5 %all_to_all.10.refs_0_ = bf16[16,1168,128]{2,1,0:T(8,128)(2,1)} all-to-all(bf16[16,1168,128]{2,1,0:T(8,128)(2,1)} %get-tuple-element.30), channel_id=1, replica_groups=mesh['zh'=4,'zl'=2,'y'=4,'k'=2,'x'=4] {'zl','y','k'}, dimensions={0} | all-to-all | bytes 9568256 | tf_op jit(solution)/shard_map/all_to_all | solution.py:279
  65.0 5.0 %all-to-all-start = ((bf16[16,400,128]{2,1,0:T(8,128)(2,1)}), bf16[16,400,128]{2,1,0:T(8,128)(2,1)S(1)}, u32[]{:S(2)}, u32[]{:S(2)}) async-start(bf16[16,400,128]{2,1,0:T(8,128)(2,1)} %get-tuple-element.26), calls=%async_computation | async-start | bytes 3276800 | tf_op jit(solution)/shard_map/all_to_all | solution.py:279
  70.0 14.2 %contract.3 = (f32[384,256]{1,0:T(8,128)}, f32[384,256]{1,0:T(8,128)}, f32[768,256]{1,0:T(8,128)}, f32[768,256]{1,0:T(8,128)}, f32[384,256]{1,0:T(8,128)}, /*index=5*/f32[384,256]{1,0:T(8,128)}) custom-call(bf16[16,1168,128]{2,1,0:T(8,128)(2,1)} %all_to_all.10.refs_0_, bf16[1024,8192]{1,0:T(8,128)(2,1)} %refs_1_.3), custom_call_target="tpu_custom_call" | custom-call | flops 1048576 | bytes 1048576 | tf_op jit(solution)/shard_map/contract/pallas_call | solution.py:251
  84.2 1.3 collective-permute-start
  85.5 2.0 %collective-permute-start.1 = (f32[768,256]{1,0:T(8,128)}, f32[768,256]{1,0:T(8,128)S(1)}, u32[]{:S(2)}, u32[]{:S(2)}) collective-permute-start(f32[768,256]{1,0:T(8,128)} %get-tuple-element.37), channel_id=1, source_target_pairs={{0,3},{1,0},{2,1},{3,2},{4,7},{5,4},{6,5},{7,6},{8,11},{9,8},{10,9... | collective-permute-start | bytes 2359304 | tf_op jit(solution)/shard_map/ppermute | solution.py:287
  87.5 4.3 %all-to-all-done.refs_0_ = bf16[16,400,128]{2,1,0:T(8,128)(2,1)S(1)} async-done(((bf16[16,400,128]{2,1,0:T(8,128)(2,1)}), bf16[16,400,128]{2,1,0:T(8,128)(2,1)S(1)}, u32[]{:S(2)}, u32[]{:S(2)}) %all-to-all-start) | async-done | bytes 1638432 | tf_op jit(solution)/shard_map/all_to_all | solution.py:279
  91.8 1.2 copy-done
  93.0 6.7 %contract.2 = (f32[256,256]{1,0:T(8,128)}, f32[256,256]{1,0:T(8,128)}, f32[256,256]{1,0:T(8,128)}, f32[256,256]{1,0:T(8,128)}) custom-call(bf16[16,400,128]{2,1,0:T(8,128)(2,1)} %copy-done, bf16[1024,8192]{1,0:T(8,128)(2,1)} %refs_1_.3), custom_call_target="tpu_custom_call" | custom-call | flops 1048576 | bytes 1048576 | tf_op jit(solution)/shard_map/contract/pallas_call | solution.py:251
  99.8 5.5 %collective-permute-done = f32[768,256]{1,0:T(8,128)S(1)} collective-permute-done((f32[768,256]{1,0:T(8,128)}, f32[768,256]{1,0:T(8,128)S(1)}, u32[]{:S(2)}, u32[]{:S(2)}) %collective-permute-start) | collective-permute-done | bytes 786464 | tf_op jit(solution)/shard_map/ppermute | solution.py:286
  105.3 0.1 collective-permute-start.3
  105.5 0.1 slice_add_fusion.1
  105.5 3.3 %collective-permute-start.2 = (f32[384,256]{1,0:T(8,128)S(1)}, f32[384,256]{1,0:T(8,128)S(1)}, u32[]{:S(2)}, u32[]{:S(2)}) collective-permute-start(f32[384,256]{1,0:T(8,128)S(1)} %slice_add_fusion.1), channel_id=1, source_target_pairs={{0,3},{1,0},{2,1},{3,2},{4,7},{5,4},{6,5},{7,6},{8,11},{9,8},{10,9... | collective-permute-start | bytes 1179656 | tf_op jit(solution)/shard_map/ppermute | solution.py:294
  108.8 8.2 %collective-permute-done.3 = f32[384,256]{1,0:T(8,128)S(1)} collective-permute-done((f32[384,256]{1,0:T(8,128)S(1)}, f32[384,256]{1,0:T(8,128)S(1)}, u32[]{:S(2)}, u32[]{:S(2)}) %collective-permute-start.3) | collective-permute-done | bytes 393248 | tf_op jit(solution)/shard_map/ppermute | solution.py:293
  117.0 0.1 slice_add_fusion.2
  117.1 0.1 slice_add_fusion.4
  117.2 5.6 %collective-permute-start.4 = (f32[256,256]{1,0:T(8,128)S(1)}, f32[256,256]{1,0:T(8,128)S(1)}, u32[]{:S(2)}, u32[]{:S(2)}) collective-permute-start(f32[256,256]{1,0:T(8,128)S(1)} %get-tuple-element.40), channel_id=1, source_target_pairs={{0,128},{64,192},{128,0},{192,64},{1,129},{65,193},{129,1},{193,65... | collective-permute-start | bytes 786440 | tf_op jit(solution)/shard_map/ppermute | solution.py:307
  122.9 4.1 %collective-permute-start.6 = (f32[256,256]{1,0:T(8,128)S(1)}, f32[256,256]{1,0:T(8,128)S(1)}, u32[]{:S(2)}, u32[]{:S(2)}) collective-permute-start(f32[256,256]{1,0:T(8,128)S(1)} %pad_maximum_fusion.2), channel_id=1, source_target_pairs={{0,192},{64,0},{128,64},{192,128},{1,193},{65,1},{129,65},{193,129... | collective-permute-start | bytes 786440 | tf_op jit(solution)/shard_map/ppermute | solution.py:307
  127.0 0.2 collective-permute-start.7
  127.2 3.1 %collective-permute-start.8 = (f32[256,256]{1,0:T(8,128)S(1)}, f32[256,256]{1,0:T(8,128)S(1)}, u32[]{:S(2)}, u32[]{:S(2)}) collective-permute-start(f32[256,256]{1,0:T(8,128)S(1)} %copy-done.7), channel_id=1, source_target_pairs={{0,3},{1,0},{2,1},{3,2},{4,7},{5,4},{6,5},{7,6},{8,11},{9,8},{10,9... | collective-permute-start | bytes 786440 | tf_op jit(solution)/shard_map/ppermute | solution.py:318
  130.2 5.3 %collective-permute-done.4 = f32[256,256]{1,0:T(8,128)S(1)} collective-permute-done((f32[256,256]{1,0:T(8,128)S(1)}, f32[256,256]{1,0:T(8,128)S(1)}, u32[]{:S(2)}, u32[]{:S(2)}) %collective-permute-start.4) | collective-permute-done | bytes 262176 | tf_op jit(solution)/shard_map/ppermute | solution.py:307
  135.6 1.7 %collective-permute-start.9 = (f32[256,256]{1,0:T(8,128)S(1)}, f32[256,256]{1,0:T(8,128)S(1)}, u32[]{:S(2)}, u32[]{:S(2)}) collective-permute-start(f32[256,256]{1,0:T(8,128)S(1)} %copy-done.6), channel_id=1, source_target_pairs={{0,2},{1,3},{2,0},{3,1},{4,6},{5,7},{6,4},{7,5},{8,10},{9,11},{10,... | collective-permute-start | bytes 786440 | tf_op jit(solution)/shard_map/ppermute | solution.py:319
  137.3 11.6 %collective-permute-done.5 = f32[256,256]{1,0:T(8,128)S(1)} collective-permute-done((f32[256,256]{1,0:T(8,128)S(1)}, f32[256,256]{1,0:T(8,128)S(1)}, u32[]{:S(2)}, u32[]{:S(2)}) %collective-permute-start.5) | collective-permute-done | bytes 262176 | tf_op jit(solution)/shard_map/ppermute | solution.py:307
  149.0 0.8 add_convert_fusion
  (27 shorter events, 0.2 us)
Async XLA Ops:
  65.0 26.7 %all-to-all-start = ((bf16[16,400,128]{2,1,0:T(8,128)(2,1)}), bf16[16,400,128]{2,1,0:T(8,128)(2,1)S(1)}, u32[]{:S(2)}, u32[]{:S(2)}) async-start(bf16[16,400,128]{2,1,0:T(8,128)(2,1)} %get-tuple-element.26), calls=%async_computation | async-start | bytes 3276800 | tf_op jit(solution)/shard_map/all_to_all | solution.py:279
  84.2 21.1 %collective-permute-start = (f32[768,256]{1,0:T(8,128)}, f32[768,256]{1,0:T(8,128)S(1)}, u32[]{:S(2)}, u32[]{:S(2)}) collective-permute-start(f32[768,256]{1,0:T(8,128)} %get-tuple-element.32), channel_id=1, source_target_pairs={{0,1},{1,2},{2,3},{3,0},{4,5},{5,6},{6,7},{7,4},{8,9},{9,10},{10,1... | collective-permute-start | bytes 2359304 | tf_op jit(solution)/shard_map/ppermute | solution.py:286
  85.5 19.9 %collective-permute-start.1 = (f32[768,256]{1,0:T(8,128)}, f32[768,256]{1,0:T(8,128)S(1)}, u32[]{:S(2)}, u32[]{:S(2)}) collective-permute-start(f32[768,256]{1,0:T(8,128)} %get-tuple-element.37), channel_id=1, source_target_pairs={{0,3},{1,0},{2,1},{3,2},{4,7},{5,4},{6,5},{7,6},{8,11},{9,8},{10,9... | collective-permute-start | bytes 2359304 | tf_op jit(solution)/shard_map/ppermute | solution.py:287
  91.8 1.2 copy-start
  93.0 12.3 %copy-start.4 = (f32[384,256]{1,0:T(8,128)S(1)}, f32[384,256]{1,0:T(8,128)}, u32[]{:S(2)}) copy-start(f32[384,256]{1,0:T(8,128)} %get-tuple-element.39) | copy-start | bytes 1179652
  93.0 12.5 %copy-start.3 = (f32[384,256]{1,0:T(8,128)S(1)}, f32[384,256]{1,0:T(8,128)}, u32[]{:S(2)}) copy-start(f32[384,256]{1,0:T(8,128)} %get-tuple-element.36) | copy-start | bytes 1179652
  93.0 24.0 %copy-start.2 = (f32[384,256]{1,0:T(8,128)S(1)}, f32[384,256]{1,0:T(8,128)}, u32[]{:S(2)}) copy-start(f32[384,256]{1,0:T(8,128)} %get-tuple-element.38) | copy-start | bytes 1179652
  93.0 24.1 %copy-start.1 = (f32[384,256]{1,0:T(8,128)S(1)}, f32[384,256]{1,0:T(8,128)}, u32[]{:S(2)}) copy-start(f32[384,256]{1,0:T(8,128)} %get-tuple-element.31) | copy-start | bytes 1179652
  99.7 27.3 %copy-start.8 = (f32[256,256]{1,0:T(8,128)S(1)}, f32[256,256]{1,0:T(8,128)}, u32[]{:S(2)}) copy-start(f32[256,256]{1,0:T(8,128)} %get-tuple-element.44) | copy-start | bytes 786436
  99.8 27.4 %copy-start.7 = (f32[256,256]{1,0:T(8,128)S(1)}, f32[256,256]{1,0:T(8,128)}, u32[]{:S(2)}) copy-start(f32[256,256]{1,0:T(8,128)} %get-tuple-element.45) | copy-start | bytes 786436
  99.8 35.8 %copy-start.6 = (f32[256,256]{1,0:T(8,128)S(1)}, f32[256,256]{1,0:T(8,128)}, u32[]{:S(2)}) copy-start(f32[256,256]{1,0:T(8,128)} %get-tuple-element.46) | copy-start | bytes 786436
  99.8 49.2 %copy-start.5 = (f32[256,256]{1,0:T(8,128)S(1)}, f32[256,256]{1,0:T(8,128)}, u32[]{:S(2)}) copy-start(f32[256,256]{1,0:T(8,128)} %get-tuple-element.43) | copy-start | bytes 786436
  105.3 11.6 %collective-permute-start.3 = (f32[384,256]{1,0:T(8,128)S(1)}, f32[384,256]{1,0:T(8,128)S(1)}, u32[]{:S(2)}, u32[]{:S(2)}) collective-permute-start(f32[384,256]{1,0:T(8,128)S(1)} %slice_add_fusion), channel_id=1, source_target_pairs={{0,1},{1,2},{2,3},{3,0},{4,5},{5,6},{6,7},{7,4},{8,9},{9,10},{10,1... | collective-permute-start | bytes 1179656 | tf_op jit(solution)/shard_map/ppermute | solution.py:293
  105.5 11.5 %collective-permute-start.2 = (f32[384,256]{1,0:T(8,128)S(1)}, f32[384,256]{1,0:T(8,128)S(1)}, u32[]{:S(2)}, u32[]{:S(2)}) collective-permute-start(f32[384,256]{1,0:T(8,128)S(1)} %slice_add_fusion.1), channel_id=1, source_target_pairs={{0,3},{1,0},{2,1},{3,2},{4,7},{5,4},{6,5},{7,6},{8,11},{9,8},{10,9... | collective-permute-start | bytes 1179656 | tf_op jit(solution)/shard_map/ppermute | solution.py:294
  117.2 18.4 %collective-permute-start.4 = (f32[256,256]{1,0:T(8,128)S(1)}, f32[256,256]{1,0:T(8,128)S(1)}, u32[]{:S(2)}, u32[]{:S(2)}) collective-permute-start(f32[256,256]{1,0:T(8,128)S(1)} %get-tuple-element.40), channel_id=1, source_target_pairs={{0,128},{64,192},{128,0},{192,64},{1,129},{65,193},{129,1},{193,65... | collective-permute-start | bytes 786440 | tf_op jit(solution)/shard_map/ppermute | solution.py:307
  122.9 26.1 %collective-permute-start.5 = (f32[256,256]{1,0:T(8,128)S(1)}, f32[256,256]{1,0:T(8,128)S(1)}, u32[]{:S(2)}, u32[]{:S(2)}) collective-permute-start(f32[256,256]{1,0:T(8,128)S(1)} %get-tuple-element.41), channel_id=1, source_target_pairs={{0,64},{64,128},{128,192},{192,0},{1,65},{65,129},{129,193},{193,1... | collective-permute-start | bytes 786440 | tf_op jit(solution)/shard_map/ppermute | solution.py:307
  122.9 26.1 %collective-permute-start.6 = (f32[256,256]{1,0:T(8,128)S(1)}, f32[256,256]{1,0:T(8,128)S(1)}, u32[]{:S(2)}, u32[]{:S(2)}) collective-permute-start(f32[256,256]{1,0:T(8,128)S(1)} %pad_maximum_fusion.2), channel_id=1, source_target_pairs={{0,192},{64,0},{128,64},{192,128},{1,193},{65,1},{129,65},{193,129... | collective-permute-start | bytes 786440 | tf_op jit(solution)/shard_map/ppermute | solution.py:307
  127.0 21.9 %collective-permute-start.7 = (f32[256,256]{1,0:T(8,128)S(1)}, f32[256,256]{1,0:T(8,128)S(1)}, u32[]{:S(2)}, u32[]{:S(2)}) collective-permute-start(f32[256,256]{1,0:T(8,128)S(1)} %copy-done.8), channel_id=1, source_target_pairs={{0,1},{1,2},{2,3},{3,0},{4,5},{5,6},{6,7},{7,4},{8,9},{9,10},{10,1... | collective-permute-start | bytes 786440 | tf_op jit(solution)/shard_map/ppermute | solution.py:318
  127.2 21.8 %collective-permute-start.8 = (f32[256,256]{1,0:T(8,128)S(1)}, f32[256,256]{1,0:T(8,128)S(1)}, u32[]{:S(2)}, u32[]{:S(2)}) collective-permute-start(f32[256,256]{1,0:T(8,128)S(1)} %copy-done.7), channel_id=1, source_target_pairs={{0,3},{1,0},{2,1},{3,2},{4,7},{5,4},{6,5},{7,6},{8,11},{9,8},{10,9... | collective-permute-start | bytes 786440 | tf_op jit(solution)/shard_map/ppermute | solution.py:318
  135.6 13.3 %collective-permute-start.9 = (f32[256,256]{1,0:T(8,128)S(1)}, f32[256,256]{1,0:T(8,128)S(1)}, u32[]{:S(2)}, u32[]{:S(2)}) collective-permute-start(f32[256,256]{1,0:T(8,128)S(1)} %copy-done.6), channel_id=1, source_target_pairs={{0,2},{1,3},{2,0},{3,1},{4,6},{5,7},{6,4},{7,5},{8,10},{9,11},{10,... | collective-permute-start | bytes 786440 | tf_op jit(solution)/shard_map/ppermute | solution.py:319

commit v6 on v5

--- a/solution.py
+++ b/solution.py
@@ -14,7 +14,7 @@
 DEPTH = 4
 WIDE = 4
 PARTS = 4
-ORDER = (2, 1, 3, 0)
+ORDER = (1, 3, 2, 0)
 CHUNKS = (3, 1)
 FIRST = (0, 3)
 

time: 151 us -> 154 us (1.020)
  the two profiles are of different devices: /device:TPU:32 before, /device:TPU:38 now
where the time goes in v6:
time: 154 us; the launch traced here: 152 us
  blocking collectives  61.3 us (40%)
  waiting for transfers between devices  46.3 us (30%)
  Pallas kernels  22.6 us (15%)
  starting transfers between devices  19 us (12%)
    all_to_all x1, blocking collectives, local(): lax.all_to_all(sent, ('zl', 'y', 'k'), split_axis=0, concat_axis=0, tiled...  61.3 us
    ppermute x3, waiting for transfers between devices, send(): lax.ppermute(block, 'zh', [(i, (i + away) % HIGH) for i in range(HIGH)])  21.8 us
    pallas_call x2, Pallas kernels, contract(): pl.pallas_call(kernel, out_shape=outs, in_specs=[hbm, hbm], out_specs=[vm...  19.1 us
    ppermute x1, waiting for transfers between devices, blocks(): from_low_b = lax.ppermute(next_b, 'x', up_x)  9.25 us
    ppermute x3, starting transfers between devices, send(): lax.ppermute(block, 'zh', [(i, (i + away) % HIGH) for i in range(HIGH)])  7.31 us
    all_to_all x1, waiting for transfers between devices, local(): lax.all_to_all(sent, ('zl', 'y', 'k'), split_axis=0, concat_axis=0, tiled...  7.27 us
    all_to_all x1, starting transfers between devices, local(): lax.all_to_all(sent, ('zl', 'y', 'k'), split_axis=0, concat_axis=0, tiled...  4.95 us
    pallas_call x1, Pallas kernels, route(): pl.pallas_call(route_kernel, out_shape=[jax.ShapeDtypeStruct((GROUP, bloc...  3.53 us
  transfers between devices with their start and end apart: 11, of which 7 were waited for; matrix products, arithmetic and copies ran while one was open for 0% of the time, Pallas kernels for 13%

profile of v6, /device:TPU:38, one launch (start us, length us, event | category | flops | bytes accessed | tf_op | source)
XLA Modules:
  0.0 151.6 jit_solution(14862036890256111302)
XLA Ops:
  0.0 3.5 %route.1 = (bf16[16,1168,128]{2,1,0:T(8,128)(2,1)}, bf16[16,400,128]{2,1,0:T(8,128)(2,1)}) custom-call(s32[96]{0:T(128)} %kc.1, s32[96]{0:T(128)} %jb.1, s32[96]{0:T(128)} %bitcast.1, bf16[96,128,128]{2,1,0:T(8,128)(2,1)} %tiles.1), custom_call_target="tpu_custom_call" | custom-call | bytes 8388608 | tf_op jit(solution)/shard_map/route/pallas_call | solution.py:102
  3.5 61.3 %all_to_all.10.refs_0_ = bf16[16,1168,128]{2,1,0:T(8,128)(2,1)} all-to-all(bf16[16,1168,128]{2,1,0:T(8,128)(2,1)} %get-tuple-element.30), channel_id=1, replica_groups=mesh['zh'=4,'zl'=2,'y'=4,'k'=2,'x'=4] {'zl','y','k'}, dimensions={0} | all-to-all | bytes 9568256 | tf_op jit(solution)/shard_map/all_to_all | solution.py:279
  64.8 5.0 %all-to-all-start = ((bf16[16,400,128]{2,1,0:T(8,128)(2,1)}), bf16[16,400,128]{2,1,0:T(8,128)(2,1)S(1)}, u32[]{:S(2)}, u32[]{:S(2)}) async-start(bf16[16,400,128]{2,1,0:T(8,128)(2,1)} %get-tuple-element.26), calls=%async_computation | async-start | bytes 3276800 | tf_op jit(solution)/shard_map/all_to_all | solution.py:279
  69.8 12.4 %contract.3 = (f32[384,256]{1,0:T(8,128)}, f32[384,256]{1,0:T(8,128)}, f32[768,256]{1,0:T(8,128)}, f32[768,256]{1,0:T(8,128)}, f32[384,256]{1,0:T(8,128)}, /*index=5*/f32[384,256]{1,0:T(8,128)}) custom-call(bf16[16,1168,128]{2,1,0:T(8,128)(2,1)} %all_to_all.10.refs_0_, bf16[1024,8192]{1,0:T(8,128)(2,1)} %refs_1_.3), custom_call_target="tpu_custom_call" | custom-call | flops 1048576 | bytes 1048576 | tf_op jit(solution)/shard_map/contract/pallas_call | solution.py:251
  82.1 0.8 collective-permute-start
  82.9 1.3 collective-permute-start.1
  84.2 7.3 %all-to-all-done.refs_0_ = bf16[16,400,128]{2,1,0:T(8,128)(2,1)S(1)} async-done(((bf16[16,400,128]{2,1,0:T(8,128)(2,1)}), bf16[16,400,128]{2,1,0:T(8,128)(2,1)S(1)}, u32[]{:S(2)}, u32[]{:S(2)}) %all-to-all-start) | async-done | bytes 1638432 | tf_op jit(solution)/shard_map/all_to_all | solution.py:279
  91.5 1.2 copy-done
  92.7 6.7 %contract.2 = (f32[256,256]{1,0:T(8,128)}, f32[256,256]{1,0:T(8,128)}, f32[256,256]{1,0:T(8,128)}, f32[256,256]{1,0:T(8,128)}) custom-call(bf16[16,400,128]{2,1,0:T(8,128)(2,1)} %copy-done, bf16[1024,8192]{1,0:T(8,128)(2,1)} %refs_1_.3), custom_call_target="tpu_custom_call" | custom-call | flops 1048576 | bytes 1048576 | tf_op jit(solution)/shard_map/contract/pallas_call | solution.py:251
  99.5 2.3 %collective-permute-done = f32[768,256]{1,0:T(8,128)S(1)} collective-permute-done((f32[768,256]{1,0:T(8,128)}, f32[768,256]{1,0:T(8,128)S(1)}, u32[]{:S(2)}, u32[]{:S(2)}) %collective-permute-start) | collective-permute-done | bytes 786464 | tf_op jit(solution)/shard_map/ppermute | solution.py:286
  101.9 2.5 %collective-permute-start.3 = (f32[384,256]{1,0:T(8,128)S(1)}, f32[384,256]{1,0:T(8,128)S(1)}, u32[]{:S(2)}, u32[]{:S(2)}) collective-permute-start(f32[384,256]{1,0:T(8,128)S(1)} %slice_add_fusion), channel_id=1, source_target_pairs={{0,1},{1,2},{2,3},{3,0},{4,5},{5,6},{6,7},{7,4},{8,9},{9,10},{10,1... | collective-permute-start | bytes 1179656 | tf_op jit(solution)/shard_map/ppermute | solution.py:293
  104.5 0.1 collective-permute-start.2
  104.6 9.3 %collective-permute-done.3 = f32[384,256]{1,0:T(8,128)S(1)} collective-permute-done((f32[384,256]{1,0:T(8,128)S(1)}, f32[384,256]{1,0:T(8,128)S(1)}, u32[]{:S(2)}, u32[]{:S(2)}) %collective-permute-start.3) | collective-permute-done | bytes 393248 | tf_op jit(solution)/shard_map/ppermute | solution.py:293
  113.9 0.1 slice_add_fusion.2
  113.9 3.0 %collective-permute-done.2 = f32[384,256]{1,0:T(8,128)S(1)} collective-permute-done((f32[384,256]{1,0:T(8,128)S(1)}, f32[384,256]{1,0:T(8,128)S(1)}, u32[]{:S(2)}, u32[]{:S(2)}) %collective-permute-start.2) | collective-permute-done | bytes 393248 | tf_op jit(solution)/shard_map/ppermute | solution.py:294
  117.0 0.1 slice_add_fusion.4
  117.1 0.1 collective-permute-start.4
  117.2 4.7 %collective-permute-start.5 = (f32[256,256]{1,0:T(8,128)S(1)}, f32[256,256]{1,0:T(8,128)S(1)}, u32[]{:S(2)}, u32[]{:S(2)}) collective-permute-start(f32[256,256]{1,0:T(8,128)S(1)} %get-tuple-element.41), channel_id=1, source_target_pairs={{0,192},{64,0},{128,64},{192,128},{1,193},{65,1},{129,65},{193,129... | collective-permute-start | bytes 786440 | tf_op jit(solution)/shard_map/ppermute | solution.py:307
  121.9 2.5 %collective-permute-start.6 = (f32[256,256]{1,0:T(8,128)S(1)}, f32[256,256]{1,0:T(8,128)S(1)}, u32[]{:S(2)}, u32[]{:S(2)}) collective-permute-start(f32[256,256]{1,0:T(8,128)S(1)} %pad_maximum_fusion.2), channel_id=1, source_target_pairs={{0,128},{64,192},{128,0},{192,64},{1,129},{65,193},{129,1},{193,65... | collective-permute-start | bytes 786440 | tf_op jit(solution)/shard_map/ppermute | solution.py:307
  124.5 2.0 %collective-permute-start.8 = (f32[256,256]{1,0:T(8,128)S(1)}, f32[256,256]{1,0:T(8,128)S(1)}, u32[]{:S(2)}, u32[]{:S(2)}) collective-permute-start(f32[256,256]{1,0:T(8,128)S(1)} %copy-done.7), channel_id=1, source_target_pairs={{0,3},{1,0},{2,1},{3,2},{4,7},{5,4},{6,5},{7,6},{8,11},{9,8},{10,9... | collective-permute-start | bytes 786440 | tf_op jit(solution)/shard_map/ppermute | solution.py:318
  126.5 15.2 %collective-permute-done.4 = f32[256,256]{1,0:T(8,128)S(1)} collective-permute-done((f32[256,256]{1,0:T(8,128)S(1)}, f32[256,256]{1,0:T(8,128)S(1)}, u32[]{:S(2)}, u32[]{:S(2)}) %collective-permute-start.4) | collective-permute-done | bytes 262176 | tf_op jit(solution)/shard_map/ppermute | solution.py:307
  141.7 6.7 %collective-permute-done.6 = f32[256,256]{1,0:T(8,128)S(1)} collective-permute-done((f32[256,256]{1,0:T(8,128)S(1)}, f32[256,256]{1,0:T(8,128)S(1)}, u32[]{:S(2)}, u32[]{:S(2)}) %collective-permute-start.6) | collective-permute-done | bytes 262176 | tf_op jit(solution)/shard_map/ppermute | solution.py:307
  148.3 2.6 %collective-permute-done.9 = f32[256,256]{1,0:T(8,128)S(1)} collective-permute-done((f32[256,256]{1,0:T(8,128)S(1)}, f32[256,256]{1,0:T(8,128)S(1)}, u32[]{:S(2)}, u32[]{:S(2)}) %collective-permute-start.9) | collective-permute-done | bytes 262176 | tf_op jit(solution)/shard_map/ppermute | solution.py:319
  150.9 0.8 add_convert_fusion
  (27 shorter events, 0.2 us)
Async XLA Ops:
  64.8 26.7 %all-to-all-start = ((bf16[16,400,128]{2,1,0:T(8,128)(2,1)}), bf16[16,400,128]{2,1,0:T(8,128)(2,1)S(1)}, u32[]{:S(2)}, u32[]{:S(2)}) async-start(bf16[16,400,128]{2,1,0:T(8,128)(2,1)} %get-tuple-element.26), calls=%async_computation | async-start | bytes 3276800 | tf_op jit(solution)/shard_map/all_to_all | solution.py:279
  82.1 19.7 %collective-permute-start = (f32[768,256]{1,0:T(8,128)}, f32[768,256]{1,0:T(8,128)S(1)}, u32[]{:S(2)}, u32[]{:S(2)}) collective-permute-start(f32[768,256]{1,0:T(8,128)} %get-tuple-element.32), channel_id=1, source_target_pairs={{0,1},{1,2},{2,3},{3,0},{4,5},{5,6},{6,7},{7,4},{8,9},{9,10},{10,1... | collective-permute-start | bytes 2359304 | tf_op jit(solution)/shard_map/ppermute | solution.py:286
  82.9 21.5 %collective-permute-start.1 = (f32[768,256]{1,0:T(8,128)}, f32[768,256]{1,0:T(8,128)S(1)}, u32[]{:S(2)}, u32[]{:S(2)}) collective-permute-start(f32[768,256]{1,0:T(8,128)} %get-tuple-element.37), channel_id=1, source_target_pairs={{0,3},{1,0},{2,1},{3,2},{4,7},{5,4},{6,5},{7,6},{8,11},{9,8},{10,9... | collective-permute-start | bytes 2359304 | tf_op jit(solution)/shard_map/ppermute | solution.py:287
  91.5 1.2 copy-start
  92.7 9.1 %copy-start.4 = (f32[384,256]{1,0:T(8,128)S(1)}, f32[384,256]{1,0:T(8,128)}, u32[]{:S(2)}) copy-start(f32[384,256]{1,0:T(8,128)} %get-tuple-element.39) | copy-start | bytes 1179652
  92.7 11.7 %copy-start.3 = (f32[384,256]{1,0:T(8,128)S(1)}, f32[384,256]{1,0:T(8,128)}, u32[]{:S(2)}) copy-start(f32[384,256]{1,0:T(8,128)} %get-tuple-element.36) | copy-start | bytes 1179652
  92.7 21.1 %copy-start.2 = (f32[384,256]{1,0:T(8,128)S(1)}, f32[384,256]{1,0:T(8,128)}, u32[]{:S(2)}) copy-start(f32[384,256]{1,0:T(8,128)} %get-tuple-element.38) | copy-start | bytes 1179652
  92.7 24.2 %copy-start.1 = (f32[384,256]{1,0:T(8,128)S(1)}, f32[384,256]{1,0:T(8,128)}, u32[]{:S(2)}) copy-start(f32[384,256]{1,0:T(8,128)} %get-tuple-element.31) | copy-start | bytes 1179652
  99.5 25.0 %copy-start.8 = (f32[256,256]{1,0:T(8,128)S(1)}, f32[256,256]{1,0:T(8,128)}, u32[]{:S(2)}) copy-start(f32[256,256]{1,0:T(8,128)} %get-tuple-element.44) | copy-start | bytes 786436
  99.5 24.9 %copy-start.7 = (f32[256,256]{1,0:T(8,128)S(1)}, f32[256,256]{1,0:T(8,128)}, u32[]{:S(2)}) copy-start(f32[256,256]{1,0:T(8,128)} %get-tuple-element.45) | copy-start | bytes 786436
  99.5 42.1 %copy-start.6 = (f32[256,256]{1,0:T(8,128)S(1)}, f32[256,256]{1,0:T(8,128)}, u32[]{:S(2)}) copy-start(f32[256,256]{1,0:T(8,128)} %get-tuple-element.46) | copy-start | bytes 786436
  99.5 51.4 %copy-start.5 = (f32[256,256]{1,0:T(8,128)S(1)}, f32[256,256]{1,0:T(8,128)}, u32[]{:S(2)}) copy-start(f32[256,256]{1,0:T(8,128)} %get-tuple-element.43) | copy-start | bytes 786436
  101.9 11.9 %collective-permute-start.3 = (f32[384,256]{1,0:T(8,128)S(1)}, f32[384,256]{1,0:T(8,128)S(1)}, u32[]{:S(2)}, u32[]{:S(2)}) collective-permute-start(f32[384,256]{1,0:T(8,128)S(1)} %slice_add_fusion), channel_id=1, source_target_pairs={{0,1},{1,2},{2,3},{3,0},{4,5},{5,6},{6,7},{7,4},{8,9},{9,10},{10,1... | collective-permute-start | bytes 1179656 | tf_op jit(solution)/shard_map/ppermute | solution.py:293
  104.5 12.5 %collective-permute-start.2 = (f32[384,256]{1,0:T(8,128)S(1)}, f32[384,256]{1,0:T(8,128)S(1)}, u32[]{:S(2)}, u32[]{:S(2)}) collective-permute-start(f32[384,256]{1,0:T(8,128)S(1)} %slice_add_fusion.1), channel_id=1, source_target_pairs={{0,3},{1,0},{2,1},{3,2},{4,7},{5,4},{6,5},{7,6},{8,11},{9,8},{10,9... | collective-permute-start | bytes 1179656 | tf_op jit(solution)/shard_map/ppermute | solution.py:294
  117.1 24.5 %collective-permute-start.4 = (f32[256,256]{1,0:T(8,128)S(1)}, f32[256,256]{1,0:T(8,128)S(1)}, u32[]{:S(2)}, u32[]{:S(2)}) collective-permute-start(f32[256,256]{1,0:T(8,128)S(1)} %get-tuple-element.40), channel_id=1, source_target_pairs={{0,64},{64,128},{128,192},{192,0},{1,65},{65,129},{129,193},{193,1... | collective-permute-start | bytes 786440 | tf_op jit(solution)/shard_map/ppermute | solution.py:307
  117.2 24.4 %collective-permute-start.5 = (f32[256,256]{1,0:T(8,128)S(1)}, f32[256,256]{1,0:T(8,128)S(1)}, u32[]{:S(2)}, u32[]{:S(2)}) collective-permute-start(f32[256,256]{1,0:T(8,128)S(1)} %get-tuple-element.41), channel_id=1, source_target_pairs={{0,192},{64,0},{128,64},{192,128},{1,193},{65,1},{129,65},{193,129... | collective-permute-start | bytes 786440 | tf_op jit(solution)/shard_map/ppermute | solution.py:307
  121.9 26.4 %collective-permute-start.6 = (f32[256,256]{1,0:T(8,128)S(1)}, f32[256,256]{1,0:T(8,128)S(1)}, u32[]{:S(2)}, u32[]{:S(2)}) collective-permute-start(f32[256,256]{1,0:T(8,128)S(1)} %pad_maximum_fusion.2), channel_id=1, source_target_pairs={{0,128},{64,192},{128,0},{192,64},{1,129},{65,193},{129,1},{193,65... | collective-permute-start | bytes 786440 | tf_op jit(solution)/shard_map/ppermute | solution.py:307
  124.4 23.9 %collective-permute-start.7 = (f32[256,256]{1,0:T(8,128)S(1)}, f32[256,256]{1,0:T(8,128)S(1)}, u32[]{:S(2)}, u32[]{:S(2)}) collective-permute-start(f32[256,256]{1,0:T(8,128)S(1)} %copy-done.8), channel_id=1, source_target_pairs={{0,1},{1,2},{2,3},{3,0},{4,5},{5,6},{6,7},{7,4},{8,9},{9,10},{10,1... | collective-permute-start | bytes 786440 | tf_op jit(solution)/shard_map/ppermute | solution.py:318
  124.5 23.9 %collective-permute-start.8 = (f32[256,256]{1,0:T(8,128)S(1)}, f32[256,256]{1,0:T(8,128)S(1)}, u32[]{:S(2)}, u32[]{:S(2)}) collective-permute-start(f32[256,256]{1,0:T(8,128)S(1)} %copy-done.7), channel_id=1, source_target_pairs={{0,3},{1,0},{2,1},{3,2},{4,7},{5,4},{6,5},{7,6},{8,11},{9,8},{10,9... | collective-permute-start | bytes 786440 | tf_op jit(solution)/shard_map/ppermute | solution.py:318
  141.6 9.2 %collective-permute-start.9 = (f32[256,256]{1,0:T(8,128)S(1)}, f32[256,256]{1,0:T(8,128)S(1)}, u32[]{:S(2)}, u32[]{:S(2)}) collective-permute-start(f32[256,256]{1,0:T(8,128)S(1)} %copy-done.6), channel_id=1, source_target_pairs={{0,2},{1,3},{2,0},{3,1},{4,6},{5,7},{6,4},{7,5},{8,10},{9,11},{10,... | collective-permute-start | bytes 786440 | tf_op jit(solution)/shard_map/ppermute | solution.py:319
